TPU v7x, 512 devices: a whole 4x4x16 slice. The times are simulated.
512 devices in a mesh: ctx: 128 (over z, y, core), head: 4 (over x).
Axes of the slice: x: 4, y: 4, z: 16, core: 2. Of those that a mesh axis runs over, the one named last changes fastest.
Arguments:
- inputs: bfloat16 [16384, 3584], P('ctx', 'head'), may hold values from -9 to 9
- queries: bfloat16 [16384, 3584], P('ctx', 'head'), may hold values from -8 to 8
- w_key: bfloat16 [3584, 512], P(None, 'head'), may hold values from -1.5 to 1.5
- w_value: bfloat16 [3584, 512], P(None, 'head'), may hold values from -0.09375 to 0.09375
- v_bias: bfloat16 [512], P('head'), may hold values from -6 to 6
- cotangent: bfloat16 [16384, 3584], P('ctx', 'head'), may hold values from -96 to 96
Outputs:
- attended: bfloat16 [16384, 3584], P('ctx', 'head')
- query_grad: bfloat16 [16384, 3584], P('ctx', 'head')
- input_grad: bfloat16 [16384, 3584], P('ctx', 'head')
All inputs are finite; a program needn't handle non-finite values.
Results may differ from a plain program's by a relative error of at most 0.025.
Values may be sent and summed in bfloat16 or wider, within the bound.
No kernel may reach another device: no remote copies, remote signals or barrier semaphores. Data moves between devices by JAX's collectives and lax.ppermute only.
A program may use at most 64 MiB of HBM per device.

v0:
```python
import math

import jax
import jax.numpy as jnp
from jax import lax
from jax.sharding import PartitionSpec as P

HEAD_DIM = 128
BLOCK = 128


def from_behind(value, axis, steps):
    count = lax.axis_size(axis)
    leading, last = (max(0, -steps), min(count, count - steps))
    return lax.ppermute(value, axis, [(source, source + steps) for source in range(leading, last)])


def masked_scores(query_rows, key_rows, allowed):
    scaled = jnp.einsum(
        "qgrd,lkgd->grqlk", query_rows, key_rows, preferred_element_type=jnp.float32
    ) * (1.0 / math.sqrt(HEAD_DIM))
    return jnp.where(allowed, scaled, -jnp.inf)


def level_stack(own_rows, fetched_rows, per_dev, row_width):
    own_blocks = own_rows.reshape(per_dev, BLOCK, row_width)
    prior_blocks = fetched_rows[0].reshape(per_dev, BLOCK, row_width)
    joined = jnp.concatenate([prior_blocks, own_blocks], axis=0)
    level_parts = [own_blocks]
    stride = 1
    while stride < per_dev:
        level_parts.append(joined[per_dev - stride : 2 * per_dev - stride])
        stride = stride * 2
    for remote_rows in fetched_rows:
        level_parts.append(remote_rows.reshape(per_dev, BLOCK, row_width))
    return jnp.stack(level_parts, axis=1)


def shards(inputs, queries, w_key, w_value, v_bias, cotangent):
    token_count = queries.shape[0]
    per_dev = token_count // BLOCK
    kv_width = w_key.shape[1]
    kv_heads = kv_width // HEAD_DIM
    group_size = queries.shape[1] // kv_width
    ctx_count = lax.axis_size("ctx")
    device_row = lax.axis_index("ctx")
    contract = (((1,), (1,)), ((), ()))
    shard_part = lax.all_gather(inputs, "head", axis=1, tiled=True)
    key_acc = jnp.dot(shard_part, w_key, preferred_element_type=jnp.float32)
    value_acc = jnp.dot(shard_part, w_value, preferred_element_type=jnp.float32)
    keys_here = key_acc.astype(jnp.bfloat16)
    values_here = (value_acc + v_bias.astype(jnp.float32)).astype(jnp.bfloat16)
    strides = [1 << bit_pos for bit_pos in range(ctx_count.bit_length() - 1)]
    fetched = [from_behind((keys_here, values_here), "ctx", stride) for stride in strides]
    near_strides = []
    stride = 1
    while stride < per_dev:
        near_strides.append(stride)
        stride = stride * 2
    distances = [0] + near_strides + [per_dev * device_step for device_step in strides]
    level_count = len(distances)
    offsets = jnp.array(distances, dtype=jnp.int32)
    global_blocks = device_row * per_dev + jnp.arange(per_dev, dtype=jnp.int32)
    valid_mask = global_blocks[:, None] - offsets[None, :] >= 0
    causal = jnp.arange(BLOCK)[:, None] >= jnp.arange(BLOCK)[None, :]
    first_level = (jnp.arange(level_count) == 0)[None, :, None]

    def stacked(fetched_pairs):
        key_levels = level_stack(
            keys_here, [pair_item[0] for pair_item in fetched_pairs], per_dev, kv_width
        )
        value_levels = level_stack(
            values_here, [pair_item[1] for pair_item in fetched_pairs], per_dev, kv_width
        )
        shape_levels = (per_dev, level_count, BLOCK, kv_heads, HEAD_DIM)
        return (key_levels.reshape(shape_levels), value_levels.reshape(shape_levels))

    key_levels, value_levels = stacked(fetched)
    query_blocks = queries.reshape(per_dev, BLOCK, kv_heads, group_size, HEAD_DIM)
    grad_blocks = cotangent.reshape(per_dev, BLOCK, kv_heads, group_size, HEAD_DIM)

    def allowed_for(valid_row):
        return jnp.where(first_level, causal[:, None, :], valid_row[None, :, None])

    def forward(packed):
        query_rows, key_rows, value_rows, valid_row = packed
        scores = masked_scores(query_rows, key_rows, allowed_for(valid_row))
        row_top = jnp.max(scores, axis=(3, 4), keepdims=True)
        log_total = row_top + jnp.log(
            jnp.sum(jnp.exp(scores - row_top), axis=(3, 4), keepdims=True)
        )
        weights = jnp.exp(scores - log_total).astype(jnp.bfloat16)
        attended = jnp.einsum(
            "grqlk,lkgd->qgrd", weights, value_rows, preferred_element_type=jnp.float32
        ).astype(jnp.bfloat16)
        return (attended, log_total)

    attended_blocks, log_totals = lax.map(
        forward, (query_blocks, key_levels, value_levels, valid_mask)
    )
    fetched_again = [from_behind((keys_here, values_here), "ctx", stride) for stride in strides]
    key_back, value_back = stacked(fetched_again)

    def backward(packed):
        query_rows, grad_rows, key_rows, value_rows, valid_row, attended_rows, log_total = packed
        scores = masked_scores(query_rows, key_rows, allowed_for(valid_row))
        prob_rows = jnp.exp(scores - log_total)
        weights = prob_rows.astype(jnp.bfloat16)
        deltas = jnp.einsum(
            "qgrd,qgrd->grq", grad_rows, attended_rows, preferred_element_type=jnp.float32
        )
        dprobs = jnp.einsum(
            "qgrd,lkgd->grqlk", grad_rows, value_rows, preferred_element_type=jnp.float32
        )
        dscores = (prob_rows * (dprobs - deltas[:, :, :, None, None])).astype(jnp.bfloat16)
        inverse_root = 1.0 / math.sqrt(HEAD_DIM)
        query_grad = (
            jnp.einsum("grqlk,lkgd->qgrd", dscores, key_rows, preferred_element_type=jnp.float32)
            * inverse_root
        ).astype(jnp.bfloat16)
        key_grad = (
            jnp.einsum("grqlk,qgrd->lkgd", dscores, query_rows, preferred_element_type=jnp.float32)
            * inverse_root
        )
        value_grad = jnp.einsum(
            "grqlk,qgrd->lkgd", weights, grad_rows, preferred_element_type=jnp.float32
        )
        return (query_grad, key_grad, value_grad)

    query_grads, key_grads, value_grads = lax.map(
        backward,
        (query_blocks, grad_blocks, key_back, value_back, valid_mask, attended_blocks, log_totals),
    )

    def settle(level_grads):
        by_level = level_grads.reshape(per_dev, level_count, BLOCK, kv_width)
        local_sum = by_level[:, 0]
        outgoing = [
            by_level[:, 1 + len(near_strides) + position] for position in range(len(strides))
        ]
        outgoing[0] = outgoing[0]
        return (
            local_sum.reshape(token_count, kv_width),
            [piece_out.reshape(token_count, kv_width) for piece_out in outgoing],
        )

    key_sum, key_out = settle(key_grads)
    value_sum, value_out = settle(value_grads)
    returned = [
        (
            from_behind(key_out[position].astype(jnp.bfloat16), "ctx", -strides[position]).astype(
                jnp.float32
            ),
            from_behind(value_out[position].astype(jnp.bfloat16), "ctx", -strides[position]).astype(
                jnp.float32
            ),
        )
        for position in range(len(strides))
    ]
    for arrived in returned:
        key_sum = key_sum + arrived[0]
        value_sum = value_sum + arrived[1]
    key_final = key_sum.astype(jnp.bfloat16)
    value_final = value_sum.astype(jnp.bfloat16)
    partial_terms = lax.dot_general(key_final, w_key, contract, preferred_element_type=jnp.float32)
    partial_terms = partial_terms + lax.dot_general(
        value_final, w_value, contract, preferred_element_type=jnp.float32
    )
    input_grad = lax.psum_scatter(
        partial_terms.astype(jnp.bfloat16), "head", scatter_dimension=1, tiled=True
    )
    attended_out = attended_blocks.reshape(token_count, queries.shape[1])
    query_out = query_grads.reshape(token_count, queries.shape[1])
    return (attended_out, query_out, input_grad)


def solution(mesh):
    return jax.shard_map(
        shards,
        mesh=mesh,
        in_specs=(
            P("ctx", "head"),
            P("ctx", "head"),
            P(None, "head"),
            P(None, "head"),
            P("head"),
            P("ctx", "head"),
        ),
        out_specs=(P("ctx", "head"), P("ctx", "head"), P("ctx", "head")),
        check_vma=False,
    )
```

profile of v0, /device:TPU:8, one launch (start us, length us, event | category | flops | bytes accessed | tf_op | source)
XLA Modules:
  0.0 177.0 jit_solution(13187595335420800183)
XLA Ops:
  7.2 0.0 copy-start
  7.2 0.0 reduce-scatter.4.cloned.1.call-start
  7.2 15.0 %all_gather.3 = bf16[128,3584]{1,0:T(8,128)(2,1)S(1)} all-gather(bf16[128,896]{1,0:T(8,128)(2,1)} %param.7), channel_id=1, replica_groups=mesh['ctx'=128,'head'=4] {'head'}, dimensions={1}, use_global_device_ids=true | all-gather | bytes 1146880 | tf_op jit(solution)/shard_map/all_gather | solution.py:48
  22.2 1.6 constant_dynamic-update-slice_fusion.15
  23.8 1.9 %collective-permute-start.7 = (bf16[128,128]{1,0:T(8,128)(2,1)S(1)}, bf16[128,128]{1,0:T(8,128)(2,1)S(1)}, u32[]{:S(2)}, u32[]{:S(2)}) collective-permute-start(bf16[128,128]{1,0:T(8,128)(2,1)S(1)} %get-tuple-element.95), channel_id=1, source_target_pairs={{0,4},{4,8},{8,12},{12,16},{16,20},{20,24},{24,28},{28,32},{32,36}... | collective-permute-start | bytes 98312 | tf_op jit(solution)/shard_map/ppermute | solution.py:15
  25.7 3.5 %collective-permute-start.8 = (bf16[128,128]{1,0:T(8,128)(2,1)S(1)}, bf16[128,128]{1,0:T(8,128)(2,1)S(1)}, u32[]{:S(2)}, u32[]{:S(2)}) collective-permute-start(bf16[128,128]{1,0:T(8,128)(2,1)S(1)} %get-tuple-element.95), channel_id=1, source_target_pairs={{0,8},{4,12},{8,16},{12,20},{16,24},{20,28},{24,32},{28,36},{32,40... | collective-permute-start | bytes 98312 | tf_op jit(solution)/shard_map/ppermute | solution.py:15
  29.2 4.2 %collective-permute-start.9 = (bf16[128,128]{1,0:T(8,128)(2,1)S(1)}, bf16[128,128]{1,0:T(8,128)(2,1)S(1)}, u32[]{:S(2)}, u32[]{:S(2)}) collective-permute-start(bf16[128,128]{1,0:T(8,128)(2,1)S(1)} %get-tuple-element.95), channel_id=1, source_target_pairs={{0,16},{4,20},{8,24},{12,28},{16,32},{20,36},{24,40},{28,44},{32,4... | collective-permute-start | bytes 98312 | tf_op jit(solution)/shard_map/ppermute | solution.py:15
  33.4 3.8 %collective-permute-start.10 = (bf16[128,128]{1,0:T(8,128)(2,1)S(1)}, bf16[128,128]{1,0:T(8,128)(2,1)S(1)}, u32[]{:S(2)}, u32[]{:S(2)}) collective-permute-start(bf16[128,128]{1,0:T(8,128)(2,1)S(1)} %get-tuple-element.95), channel_id=1, source_target_pairs={{0,32},{4,36},{8,40},{12,44},{16,48},{20,52},{24,56},{28,60},{32,6... | collective-permute-start | bytes 98312 | tf_op jit(solution)/shard_map/ppermute | solution.py:15
  37.2 6.4 %collective-permute-start.11 = (bf16[128,128]{1,0:T(8,128)(2,1)S(1)}, bf16[128,128]{1,0:T(8,128)(2,1)S(1)}, u32[]{:S(2)}, u32[]{:S(2)}) collective-permute-start(bf16[128,128]{1,0:T(8,128)(2,1)S(1)} %get-tuple-element.95), channel_id=1, source_target_pairs={{0,64},{4,68},{8,72},{12,76},{16,80},{20,84},{24,88},{28,92},{32,9... | collective-permute-start | bytes 98312 | tf_op jit(solution)/shard_map/ppermute | solution.py:15
  43.7 0.7 convert_element_type.146
  44.3 0.7 add_compare_fusion
  45.0 1.0 constant_dynamic-update-slice_fusion.7
  46.0 0.1 broadcast_select_fusion
  46.1 0.2 copy.36
  46.3 0.0 copy-start.5
  46.3 0.2 copy.32
  46.5 9.1 %collective-permute-start.12 = (bf16[128,128]{1,0:T(8,128)(2,1)S(1)}, bf16[128,128]{1,0:T(8,128)(2,1)S(1)}, u32[]{:S(2)}, u32[]{:S(2)}) collective-permute-start(bf16[128,128]{1,0:T(8,128)(2,1)S(1)} %get-tuple-element.95), channel_id=1, source_target_pairs={{0,128},{4,132},{8,136},{12,140},{16,144},{20,148},{24,152},{28,15... | collective-permute-start | bytes 98312 | tf_op jit(solution)/shard_map/ppermute | solution.py:15
  55.7 5.1 %collective-permute-start.13 = (bf16[128,128]{1,0:T(8,128)(2,1)S(1)}, bf16[128,128]{1,0:T(8,128)(2,1)S(1)}, u32[]{:S(2)}, u32[]{:S(2)}) collective-permute-start(bf16[128,128]{1,0:T(8,128)(2,1)S(1)} %get-tuple-element.95), channel_id=1, source_target_pairs={{0,256},{4,260},{8,264},{12,268},{16,272},{20,276},{24,280},{28,28... | collective-permute-start | bytes 98312 | tf_op jit(solution)/shard_map/ppermute | solution.py:15
  60.8 2.2 %collective-permute-start = (bf16[128,128]{1,0:T(8,128)(2,1)S(1)}, bf16[128,128]{1,0:T(8,128)(2,1)S(1)}, u32[]{:S(2)}, u32[]{:S(2)}) collective-permute-start(bf16[128,128]{1,0:T(8,128)(2,1)S(1)} %get-tuple-element.93), channel_id=1, source_target_pairs={{0,4},{4,8},{8,12},{12,16},{16,20},{20,24},{24,28},{28,32},{32,36}... | collective-permute-start | bytes 98312 | tf_op jit(solution)/shard_map/ppermute | solution.py:15
  63.0 0.0 collective-permute-done.10
  63.0 2.9 %collective-permute-start.1 = (bf16[128,128]{1,0:T(8,128)(2,1)S(1)}, bf16[128,128]{1,0:T(8,128)(2,1)S(1)}, u32[]{:S(2)}, u32[]{:S(2)}) collective-permute-start(bf16[128,128]{1,0:T(8,128)(2,1)S(1)} %get-tuple-element.93), channel_id=1, source_target_pairs={{0,8},{4,12},{8,16},{12,20},{16,24},{20,28},{24,32},{28,36},{32,40... | collective-permute-start | bytes 98312 | tf_op jit(solution)/shard_map/ppermute | solution.py:15
  65.9 4.7 %collective-permute-start.2 = (bf16[128,128]{1,0:T(8,128)(2,1)S(1)}, bf16[128,128]{1,0:T(8,128)(2,1)S(1)}, u32[]{:S(2)}, u32[]{:S(2)}) collective-permute-start(bf16[128,128]{1,0:T(8,128)(2,1)S(1)} %get-tuple-element.93), channel_id=1, source_target_pairs={{0,16},{4,20},{8,24},{12,28},{16,32},{20,36},{24,40},{28,44},{32,4... | collective-permute-start | bytes 98312 | tf_op jit(solution)/shard_map/ppermute | solution.py:15
  70.6 0.0 collective-permute-done.12
  70.7 2.3 %collective-permute-start.3 = (bf16[128,128]{1,0:T(8,128)(2,1)S(1)}, bf16[128,128]{1,0:T(8,128)(2,1)S(1)}, u32[]{:S(2)}, u32[]{:S(2)}) collective-permute-start(bf16[128,128]{1,0:T(8,128)(2,1)S(1)} %get-tuple-element.93), channel_id=1, source_target_pairs={{0,32},{4,36},{8,40},{12,44},{16,48},{20,52},{24,56},{28,60},{32,6... | collective-permute-start | bytes 98312 | tf_op jit(solution)/shard_map/ppermute | solution.py:15
  73.0 0.0 collective-permute-done.13
  73.0 2.5 %collective-permute-start.4 = (bf16[128,128]{1,0:T(8,128)(2,1)S(1)}, bf16[128,128]{1,0:T(8,128)(2,1)S(1)}, u32[]{:S(2)}, u32[]{:S(2)}) collective-permute-start(bf16[128,128]{1,0:T(8,128)(2,1)S(1)} %get-tuple-element.93), channel_id=1, source_target_pairs={{0,64},{4,68},{8,72},{12,76},{16,80},{20,84},{24,88},{28,92},{32,9... | collective-permute-start | bytes 98312 | tf_op jit(solution)/shard_map/ppermute | solution.py:15
  75.5 0.7 fusion.4
  76.1 0.8 exponential_reduce_fusion
  76.9 1.0 fusion.57
  77.9 0.0 collective-permute-done
  77.9 2.5 %collective-permute-start.5 = (bf16[128,128]{1,0:T(8,128)(2,1)S(1)}, bf16[128,128]{1,0:T(8,128)(2,1)S(1)}, u32[]{:S(2)}, u32[]{:S(2)}) collective-permute-start(bf16[128,128]{1,0:T(8,128)(2,1)S(1)} %get-tuple-element.93), channel_id=1, source_target_pairs={{0,128},{4,132},{8,136},{12,140},{16,144},{20,148},{24,152},{28,15... | collective-permute-start | bytes 98312 | tf_op jit(solution)/shard_map/ppermute | solution.py:15
  80.4 2.5 %collective-permute-start.6 = (bf16[128,128]{1,0:T(8,128)(2,1)S(1)}, bf16[128,128]{1,0:T(8,128)(2,1)S(1)}, u32[]{:S(2)}, u32[]{:S(2)}) collective-permute-start(bf16[128,128]{1,0:T(8,128)(2,1)S(1)} %get-tuple-element.93), channel_id=1, source_target_pairs={{0,256},{4,260},{8,264},{12,268},{16,272},{20,276},{24,280},{28,28... | collective-permute-start | bytes 98312 | tf_op jit(solution)/shard_map/ppermute | solution.py:15
  83.0 1.5 collective-permute-done.6
  84.5 1.7 fusion.30
  86.2 2.2 %fusion.2 = bf16[1,7,128,8,128]{2,4,1,3,0:T(8,128)(2,1)S(1)} fusion(f32[8,128,128,7]{2,1,3,0:T(8,128)S(1)} %get-tuple-element.97, bf16[128,7,128,1]{0,2,1,3:T(8,128)(2,1)} %bitcast.268, f32[7,128]{1,0:T(8,128)S(1)} %get-tuple-element.98, f32[7,128]{1,0:T(8,128)S(1)} %log_add_fusion, pred[128,8,128]{0,2,1:T(8,128)(4,1)S(1)} %broadcast_select_fusion, ...), kind=kOutput, calls=%fused_computation.4 | convolution fusion | flops 240386048 | bytes 6134784 | tf_op jit(solution)/shard_map/while/body/eval_jaxpr/qgrd,lkgd->grqlk/dot_general | solution.py:112
  88.4 0.0 copy-start.1
  88.4 1.4 collective-permute-start.27
  89.9 1.3 collective-permute-start.26
  91.2 1.3 collective-permute-start.25
  92.5 1.3 collective-permute-start.24
  93.8 1.3 collective-permute-start.23
  95.1 0.6 fusion.58
  95.7 7.3 %collective-permute-done.27 = bf16[128,128]{1,0:T(8,128)(2,1)S(1)} collective-permute-done((bf16[128,128]{1,0:T(8,128)(2,1)S(1)}, bf16[128,128]{1,0:T(8,128)(2,1)S(1)}, u32[]{:S(2)}, u32[]{:S(2)}) %collective-permute-start.27) | collective-permute-done | bytes 32800 | tf_op jit(solution)/shard_map/ppermute | solution.py:15
  103.1 3.6 %collective-permute-start.22 = (bf16[128,128]{1,0:T(8,128)(2,1)S(1)}, bf16[128,128]{1,0:T(8,128)(2,1)S(1)}, u32[]{:S(2)}, u32[]{:S(2)}) collective-permute-start(bf16[128,128]{1,0:T(8,128)(2,1)S(1)} %get-tuple-element.91), channel_id=1, source_target_pairs={{8,0},{12,4},{16,8},{20,12},{24,16},{28,20},{32,24},{36,28},{40,32... | collective-permute-start | bytes 98312 | tf_op jit(solution)/shard_map/ppermute | solution.py:15
  106.7 1.9 %collective-permute-start.21 = (bf16[128,128]{1,0:T(8,128)(2,1)S(1)}, bf16[128,128]{1,0:T(8,128)(2,1)S(1)}, u32[]{:S(2)}, u32[]{:S(2)}) collective-permute-start(bf16[128,128]{1,0:T(8,128)(2,1)S(1)} %get-tuple-element.72), channel_id=1, source_target_pairs={{4,0},{8,4},{12,8},{16,12},{20,16},{24,20},{28,24},{32,28},{36,32}... | collective-permute-start | bytes 98312 | tf_op jit(solution)/shard_map/ppermute | solution.py:15
  108.6 1.3 collective-permute-start.20
  109.9 1.3 collective-permute-start.19
  111.2 1.3 collective-permute-start.18
  112.5 1.3 collective-permute-start.17
  113.9 1.3 collective-permute-start.16
  115.2 8.0 %collective-permute-done.20 = bf16[128,128]{1,0:T(8,128)(2,1)S(1)} collective-permute-done((bf16[128,128]{1,0:T(8,128)(2,1)S(1)}, bf16[128,128]{1,0:T(8,128)(2,1)S(1)}, u32[]{:S(2)}, u32[]{:S(2)}) %collective-permute-start.20) | collective-permute-done | bytes 32800 | tf_op jit(solution)/shard_map/ppermute | solution.py:15
  123.1 1.9 %collective-permute-start.15 = (bf16[128,128]{1,0:T(8,128)(2,1)S(1)}, bf16[128,128]{1,0:T(8,128)(2,1)S(1)}, u32[]{:S(2)}, u32[]{:S(2)}) collective-permute-start(bf16[128,128]{1,0:T(8,128)(2,1)S(1)} %get-tuple-element.71), channel_id=1, source_target_pairs={{8,0},{12,4},{16,8},{20,12},{24,16},{28,20},{32,24},{36,28},{40,32... | collective-permute-start | bytes 98312 | tf_op jit(solution)/shard_map/ppermute | solution.py:15
  125.1 1.9 %collective-permute-start.14 = (bf16[128,128]{1,0:T(8,128)(2,1)S(1)}, bf16[128,128]{1,0:T(8,128)(2,1)S(1)}, u32[]{:S(2)}, u32[]{:S(2)}) collective-permute-start(bf16[128,128]{1,0:T(8,128)(2,1)S(1)} %get-tuple-element.65), channel_id=1, source_target_pairs={{4,0},{8,4},{12,8},{16,12},{20,16},{24,20},{28,24},{32,28},{36,32}... | collective-permute-start | bytes 98312 | tf_op jit(solution)/shard_map/ppermute | solution.py:15
  127.0 0.4 fusion.53
  127.4 0.0 copy-start.4
  127.4 1.5 collective-permute-done.15
  128.9 1.4 fusion
  130.3 2.2 %copy.74 = bf16[128,3584]{0,1:T(8,128)(2,1)} copy(bf16[128,3584]{1,0:T(8,128)(2,1)} %fusion) | data formatting | bytes 1835008
  132.5 0.0 reduce-scatter.4.cloned.1.call-update
  132.6 0.8 copy.42
  133.4 0.5 fusion.25
  133.9 0.8 copy.43
  134.7 33.7 %reduce-scatter.4.cloned.1.call-done = bf16[896,128]{1,0:T(8,128)(2,1)} async-done(((bf16[3584,128]{1,0:T(8,128)(2,1)}), bf16[896,128]{1,0:T(8,128)(2,1)}) %reduce-scatter.4.cloned.1.call-update) | async-done | bytes 229392
  168.4 1.8 copy.75
  (48 shorter events, 0.3 us)
Async XLA Ops:
  7.2 37.8 %copy-start = (bf16[3584,128]{1,0:T(8,128)(2,1)S(1)}, bf16[3584,128]{1,0:T(8,128)(2,1)}, u32[]{:S(2)}) copy-start(bf16[3584,128]{1,0:T(8,128)(2,1)} %param.10) | copy-start | bytes 2752516
  7.2 39.0 %copy-start.2 = (bf16[128,896]{1,0:T(8,128)(2,1)S(1)}, bf16[128,896]{1,0:T(8,128)(2,1)}, u32[]{:S(2)}) copy-start(bf16[128,896]{1,0:T(8,128)(2,1)} %param.12) | copy-start | bytes 688132
  7.2 39.1 %copy-start.3 = (bf16[128,896]{1,0:T(8,128)(2,1)S(1)}, bf16[128,896]{1,0:T(8,128)(2,1)}, u32[]{:S(2)}) copy-start(bf16[128,896]{1,0:T(8,128)(2,1)} %param.8) | copy-start | bytes 688132
  7.2 161.2 %reduce-scatter.4.cloned.1.call-start = ((), (), s32[]{:S(2)}) async-start(), calls=%async_computation.1 | async-start | bytes 1146880
  23.8 22.7 %collective-permute-start.7 = (bf16[128,128]{1,0:T(8,128)(2,1)S(1)}, bf16[128,128]{1,0:T(8,128)(2,1)S(1)}, u32[]{:S(2)}, u32[]{:S(2)}) collective-permute-start(bf16[128,128]{1,0:T(8,128)(2,1)S(1)} %get-tuple-element.95), channel_id=1, source_target_pairs={{0,4},{4,8},{8,12},{12,16},{16,20},{20,24},{24,28},{28,32},{32,36}... | collective-permute-start | bytes 98312 | tf_op jit(solution)/shard_map/ppermute | solution.py:15
  25.7 29.9 %collective-permute-start.8 = (bf16[128,128]{1,0:T(8,128)(2,1)S(1)}, bf16[128,128]{1,0:T(8,128)(2,1)S(1)}, u32[]{:S(2)}, u32[]{:S(2)}) collective-permute-start(bf16[128,128]{1,0:T(8,128)(2,1)S(1)} %get-tuple-element.95), channel_id=1, source_target_pairs={{0,8},{4,12},{8,16},{12,20},{16,24},{20,28},{24,32},{28,36},{32,40... | collective-permute-start | bytes 98312 | tf_op jit(solution)/shard_map/ppermute | solution.py:15
  29.2 31.6 %collective-permute-start.9 = (bf16[128,128]{1,0:T(8,128)(2,1)S(1)}, bf16[128,128]{1,0:T(8,128)(2,1)S(1)}, u32[]{:S(2)}, u32[]{:S(2)}) collective-permute-start(bf16[128,128]{1,0:T(8,128)(2,1)S(1)} %get-tuple-element.95), channel_id=1, source_target_pairs={{0,16},{4,20},{8,24},{12,28},{16,32},{20,36},{24,40},{28,44},{32,4... | collective-permute-start | bytes 98312 | tf_op jit(solution)/shard_map/ppermute | solution.py:15
  33.4 29.6 %collective-permute-start.10 = (bf16[128,128]{1,0:T(8,128)(2,1)S(1)}, bf16[128,128]{1,0:T(8,128)(2,1)S(1)}, u32[]{:S(2)}, u32[]{:S(2)}) collective-permute-start(bf16[128,128]{1,0:T(8,128)(2,1)S(1)} %get-tuple-element.95), channel_id=1, source_target_pairs={{0,32},{4,36},{8,40},{12,44},{16,48},{20,52},{24,56},{28,60},{32,6... | collective-permute-start | bytes 98312 | tf_op jit(solution)/shard_map/ppermute | solution.py:15
  37.2 28.7 %collective-permute-start.11 = (bf16[128,128]{1,0:T(8,128)(2,1)S(1)}, bf16[128,128]{1,0:T(8,128)(2,1)S(1)}, u32[]{:S(2)}, u32[]{:S(2)}) collective-permute-start(bf16[128,128]{1,0:T(8,128)(2,1)S(1)} %get-tuple-element.95), channel_id=1, source_target_pairs={{0,64},{4,68},{8,72},{12,76},{16,80},{20,84},{24,88},{28,92},{32,9... | collective-permute-start | bytes 98312 | tf_op jit(solution)/shard_map/ppermute | solution.py:15
  46.3 38.2 %copy-start.5 = (bf16[128,896]{0,1:T(8,128)(2,1)}, bf16[128,896]{0,1:T(8,128)(2,1)S(1)}, u32[]{:S(2)}) copy-start(bf16[128,896]{0,1:T(8,128)(2,1)S(1)} %copy.36) | copy-start | bytes 688132
  46.5 24.1 %collective-permute-start.12 = (bf16[128,128]{1,0:T(8,128)(2,1)S(1)}, bf16[128,128]{1,0:T(8,128)(2,1)S(1)}, u32[]{:S(2)}, u32[]{:S(2)}) collective-permute-start(bf16[128,128]{1,0:T(8,128)(2,1)S(1)} %get-tuple-element.95), channel_id=1, source_target_pairs={{0,128},{4,132},{8,136},{12,140},{16,144},{20,148},{24,152},{28,15... | collective-permute-start | bytes 98312 | tf_op jit(solution)/shard_map/ppermute | solution.py:15
  55.7 17.3 %collective-permute-start.13 = (bf16[128,128]{1,0:T(8,128)(2,1)S(1)}, bf16[128,128]{1,0:T(8,128)(2,1)S(1)}, u32[]{:S(2)}, u32[]{:S(2)}) collective-permute-start(bf16[128,128]{1,0:T(8,128)(2,1)S(1)} %get-tuple-element.95), channel_id=1, source_target_pairs={{0,256},{4,260},{8,264},{12,268},{16,272},{20,276},{24,280},{28,28... | collective-permute-start | bytes 98312 | tf_op jit(solution)/shard_map/ppermute | solution.py:15
  60.8 17.1 %collective-permute-start = (bf16[128,128]{1,0:T(8,128)(2,1)S(1)}, bf16[128,128]{1,0:T(8,128)(2,1)S(1)}, u32[]{:S(2)}, u32[]{:S(2)}) collective-permute-start(bf16[128,128]{1,0:T(8,128)(2,1)S(1)} %get-tuple-element.93), channel_id=1, source_target_pairs={{0,4},{4,8},{8,12},{12,16},{16,20},{20,24},{24,28},{28,32},{32,36}... | collective-permute-start | bytes 98312 | tf_op jit(solution)/shard_map/ppermute | solution.py:15
  63.0 17.4 %collective-permute-start.1 = (bf16[128,128]{1,0:T(8,128)(2,1)S(1)}, bf16[128,128]{1,0:T(8,128)(2,1)S(1)}, u32[]{:S(2)}, u32[]{:S(2)}) collective-permute-start(bf16[128,128]{1,0:T(8,128)(2,1)S(1)} %get-tuple-element.93), channel_id=1, source_target_pairs={{0,8},{4,12},{8,16},{12,20},{16,24},{20,28},{24,32},{28,36},{32,40... | collective-permute-start | bytes 98312 | tf_op jit(solution)/shard_map/ppermute | solution.py:15
  65.9 17.0 %collective-permute-start.2 = (bf16[128,128]{1,0:T(8,128)(2,1)S(1)}, bf16[128,128]{1,0:T(8,128)(2,1)S(1)}, u32[]{:S(2)}, u32[]{:S(2)}) collective-permute-start(bf16[128,128]{1,0:T(8,128)(2,1)S(1)} %get-tuple-element.93), channel_id=1, source_target_pairs={{0,16},{4,20},{8,24},{12,28},{16,32},{20,36},{24,40},{28,44},{32,4... | collective-permute-start | bytes 98312 | tf_op jit(solution)/shard_map/ppermute | solution.py:15
  70.7 12.3 %collective-permute-start.3 = (bf16[128,128]{1,0:T(8,128)(2,1)S(1)}, bf16[128,128]{1,0:T(8,128)(2,1)S(1)}, u32[]{:S(2)}, u32[]{:S(2)}) collective-permute-start(bf16[128,128]{1,0:T(8,128)(2,1)S(1)} %get-tuple-element.93), channel_id=1, source_target_pairs={{0,32},{4,36},{8,40},{12,44},{16,48},{20,52},{24,56},{28,60},{32,6... | collective-permute-start | bytes 98312 | tf_op jit(solution)/shard_map/ppermute | solution.py:15
  73.0 10.0 %collective-permute-start.4 = (bf16[128,128]{1,0:T(8,128)(2,1)S(1)}, bf16[128,128]{1,0:T(8,128)(2,1)S(1)}, u32[]{:S(2)}, u32[]{:S(2)}) collective-permute-start(bf16[128,128]{1,0:T(8,128)(2,1)S(1)} %get-tuple-element.93), channel_id=1, source_target_pairs={{0,64},{4,68},{8,72},{12,76},{16,80},{20,84},{24,88},{28,92},{32,9... | collective-permute-start | bytes 98312 | tf_op jit(solution)/shard_map/ppermute | solution.py:15
  76.9 3.5 %copy-start.6 = (bf16[1,8,128,128]{3,2,1,0:T(8,128)(2,1)S(1)}, bf16[1,8,128,128]{3,2,1,0:T(8,128)(2,1)}, u32[]{:S(2)}) copy-start(bf16[1,8,128,128]{3,2,1,0:T(8,128)(2,1)} %get-tuple-element.92) | copy-start | bytes 786436
  77.9 5.1 %collective-permute-start.5 = (bf16[128,128]{1,0:T(8,128)(2,1)S(1)}, bf16[128,128]{1,0:T(8,128)(2,1)S(1)}, u32[]{:S(2)}, u32[]{:S(2)}) collective-permute-start(bf16[128,128]{1,0:T(8,128)(2,1)S(1)} %get-tuple-element.93), channel_id=1, source_target_pairs={{0,128},{4,132},{8,136},{12,140},{16,144},{20,148},{24,152},{28,15... | collective-permute-start | bytes 98312 | tf_op jit(solution)/shard_map/ppermute | solution.py:15
  80.4 4.1 %collective-permute-start.6 = (bf16[128,128]{1,0:T(8,128)(2,1)S(1)}, bf16[128,128]{1,0:T(8,128)(2,1)S(1)}, u32[]{:S(2)}, u32[]{:S(2)}) collective-permute-start(bf16[128,128]{1,0:T(8,128)(2,1)S(1)} %get-tuple-element.93), channel_id=1, source_target_pairs={{0,256},{4,260},{8,264},{12,268},{16,272},{20,276},{24,280},{28,28... | collective-permute-start | bytes 98312 | tf_op jit(solution)/shard_map/ppermute | solution.py:15
  88.4 40.5 %copy-start.1 = (bf16[3584,128]{1,0:T(8,128)(2,1)S(1)}, bf16[3584,128]{1,0:T(8,128)(2,1)}, u32[]{:S(2)}) copy-start(bf16[3584,128]{1,0:T(8,128)(2,1)} %param.9) | copy-start | bytes 2752516
  88.4 14.7 %collective-permute-start.27 = (bf16[128,128]{1,0:T(8,128)(2,1)S(1)}, bf16[128,128]{1,0:T(8,128)(2,1)S(1)}, u32[]{:S(2)}, u32[]{:S(2)}) collective-permute-start(bf16[128,128]{1,0:T(8,128)(2,1)S(1)} %get-tuple-element.73), channel_id=1, source_target_pairs={{256,0},{260,4},{264,8},{268,12},{272,16},{276,20},{280,24},{284,2... | collective-permute-start | bytes 98312 | tf_op jit(solution)/shard_map/ppermute | solution.py:15
  89.9 16.8 %collective-permute-start.26 = (bf16[128,128]{1,0:T(8,128)(2,1)S(1)}, bf16[128,128]{1,0:T(8,128)(2,1)S(1)}, u32[]{:S(2)}, u32[]{:S(2)}) collective-permute-start(bf16[128,128]{1,0:T(8,128)(2,1)S(1)} %get-tuple-element.74), channel_id=1, source_target_pairs={{128,0},{132,4},{136,8},{140,12},{144,16},{148,20},{152,24},{156,2... | collective-permute-start | bytes 98312 | tf_op jit(solution)/shard_map/ppermute | solution.py:15
  91.2 17.4 %collective-permute-start.25 = (bf16[128,128]{1,0:T(8,128)(2,1)S(1)}, bf16[128,128]{1,0:T(8,128)(2,1)S(1)}, u32[]{:S(2)}, u32[]{:S(2)}) collective-permute-start(bf16[128,128]{1,0:T(8,128)(2,1)S(1)} %get-tuple-element.88), channel_id=1, source_target_pairs={{64,0},{68,4},{72,8},{76,12},{80,16},{84,20},{88,24},{92,28},{96,3... | collective-permute-start | bytes 98312 | tf_op jit(solution)/shard_map/ppermute | solution.py:15
  92.5 17.4 %collective-permute-start.24 = (bf16[128,128]{1,0:T(8,128)(2,1)S(1)}, bf16[128,128]{1,0:T(8,128)(2,1)S(1)}, u32[]{:S(2)}, u32[]{:S(2)}) collective-permute-start(bf16[128,128]{1,0:T(8,128)(2,1)S(1)} %get-tuple-element.89), channel_id=1, source_target_pairs={{32,0},{36,4},{40,8},{44,12},{48,16},{52,20},{56,24},{60,28},{64,3... | collective-permute-start | bytes 98312 | tf_op jit(solution)/shard_map/ppermute | solution.py:15
  93.8 17.5 %collective-permute-start.23 = (bf16[128,128]{1,0:T(8,128)(2,1)S(1)}, bf16[128,128]{1,0:T(8,128)(2,1)S(1)}, u32[]{:S(2)}, u32[]{:S(2)}) collective-permute-start(bf16[128,128]{1,0:T(8,128)(2,1)S(1)} %get-tuple-element.90), channel_id=1, source_target_pairs={{16,0},{20,4},{24,8},{28,12},{32,16},{36,20},{40,24},{44,28},{48,3... | collective-permute-start | bytes 98312 | tf_op jit(solution)/shard_map/ppermute | solution.py:15
  103.1 9.4 %collective-permute-start.22 = (bf16[128,128]{1,0:T(8,128)(2,1)S(1)}, bf16[128,128]{1,0:T(8,128)(2,1)S(1)}, u32[]{:S(2)}, u32[]{:S(2)}) collective-permute-start(bf16[128,128]{1,0:T(8,128)(2,1)S(1)} %get-tuple-element.91), channel_id=1, source_target_pairs={{8,0},{12,4},{16,8},{20,12},{24,16},{28,20},{32,24},{36,28},{40,32... | collective-permute-start | bytes 98312 | tf_op jit(solution)/shard_map/ppermute | solution.py:15
  106.7 7.2 %collective-permute-start.21 = (bf16[128,128]{1,0:T(8,128)(2,1)S(1)}, bf16[128,128]{1,0:T(8,128)(2,1)S(1)}, u32[]{:S(2)}, u32[]{:S(2)}) collective-permute-start(bf16[128,128]{1,0:T(8,128)(2,1)S(1)} %get-tuple-element.72), channel_id=1, source_target_pairs={{4,0},{8,4},{12,8},{16,12},{20,16},{24,20},{28,24},{32,28},{36,32}... | collective-permute-start | bytes 98312 | tf_op jit(solution)/shard_map/ppermute | solution.py:15
  108.6 14.5 %collective-permute-start.20 = (bf16[128,128]{1,0:T(8,128)(2,1)S(1)}, bf16[128,128]{1,0:T(8,128)(2,1)S(1)}, u32[]{:S(2)}, u32[]{:S(2)}) collective-permute-start(bf16[128,128]{1,0:T(8,128)(2,1)S(1)} %get-tuple-element.66), channel_id=1, source_target_pairs={{256,0},{260,4},{264,8},{268,12},{272,16},{276,20},{280,24},{284,2... | collective-permute-start | bytes 98312 | tf_op jit(solution)/shard_map/ppermute | solution.py:15
  109.9 15.1 %collective-permute-start.19 = (bf16[128,128]{1,0:T(8,128)(2,1)S(1)}, bf16[128,128]{1,0:T(8,128)(2,1)S(1)}, u32[]{:S(2)}, u32[]{:S(2)}) collective-permute-start(bf16[128,128]{1,0:T(8,128)(2,1)S(1)} %get-tuple-element.67), channel_id=1, source_target_pairs={{128,0},{132,4},{136,8},{140,12},{144,16},{148,20},{152,24},{156,2... | collective-permute-start | bytes 98312 | tf_op jit(solution)/shard_map/ppermute | solution.py:15
  111.2 16.2 %collective-permute-start.18 = (bf16[128,128]{1,0:T(8,128)(2,1)S(1)}, bf16[128,128]{1,0:T(8,128)(2,1)S(1)}, u32[]{:S(2)}, u32[]{:S(2)}) collective-permute-start(bf16[128,128]{1,0:T(8,128)(2,1)S(1)} %get-tuple-element.68), channel_id=1, source_target_pairs={{64,0},{68,4},{72,8},{76,12},{80,16},{84,20},{88,24},{92,28},{96,3... | collective-permute-start | bytes 98312 | tf_op jit(solution)/shard_map/ppermute | solution.py:15
  112.5 14.9 %collective-permute-start.17 = (bf16[128,128]{1,0:T(8,128)(2,1)S(1)}, bf16[128,128]{1,0:T(8,128)(2,1)S(1)}, u32[]{:S(2)}, u32[]{:S(2)}) collective-permute-start(bf16[128,128]{1,0:T(8,128)(2,1)S(1)} %get-tuple-element.69), channel_id=1, source_target_pairs={{32,0},{36,4},{40,8},{44,12},{48,16},{52,20},{56,24},{60,28},{64,3... | collective-permute-start | bytes 98312 | tf_op jit(solution)/shard_map/ppermute | solution.py:15
  113.9 13.6 %collective-permute-start.16 = (bf16[128,128]{1,0:T(8,128)(2,1)S(1)}, bf16[128,128]{1,0:T(8,128)(2,1)S(1)}, u32[]{:S(2)}, u32[]{:S(2)}) collective-permute-start(bf16[128,128]{1,0:T(8,128)(2,1)S(1)} %get-tuple-element.70), channel_id=1, source_target_pairs={{16,0},{20,4},{24,8},{28,12},{32,16},{36,20},{40,24},{44,28},{48,3... | collective-permute-start | bytes 98312 | tf_op jit(solution)/shard_map/ppermute | solution.py:15
  123.1 5.8 %collective-permute-start.15 = (bf16[128,128]{1,0:T(8,128)(2,1)S(1)}, bf16[128,128]{1,0:T(8,128)(2,1)S(1)}, u32[]{:S(2)}, u32[]{:S(2)}) collective-permute-start(bf16[128,128]{1,0:T(8,128)(2,1)S(1)} %get-tuple-element.71), channel_id=1, source_target_pairs={{8,0},{12,4},{16,8},{20,12},{24,16},{28,20},{32,24},{36,28},{40,32... | collective-permute-start | bytes 98312 | tf_op jit(solution)/shard_map/ppermute | solution.py:15
  125.1 3.9 %collective-permute-start.14 = (bf16[128,128]{1,0:T(8,128)(2,1)S(1)}, bf16[128,128]{1,0:T(8,128)(2,1)S(1)}, u32[]{:S(2)}, u32[]{:S(2)}) collective-permute-start(bf16[128,128]{1,0:T(8,128)(2,1)S(1)} %get-tuple-element.65), channel_id=1, source_target_pairs={{4,0},{8,4},{12,8},{16,12},{20,16},{24,20},{28,24},{32,28},{36,32}... | collective-permute-start | bytes 98312 | tf_op jit(solution)/shard_map/ppermute | solution.py:15
  127.4 5.1 %copy-start.4 = (bf16[128,7,128]{2,0,1:T(8,128)(2,1)S(1)}, bf16[128,7,128]{2,0,1:T(8,128)(2,1)}, u32[]{:S(2)}) copy-start(bf16[128,7,128]{2,0,1:T(8,128)(2,1)} %get-tuple-element.99) | copy-start | bytes 688132
Sparse Core Ops, SparseCore 0:
  132.7 35.6 reduce-scatter.3
where the time goes:
time: 178 us; the launch traced here: 177 us
  starting transfers between devices  75.9 us (43%)
  waiting for transfers between devices  52 us (29%)
  blocking collectives  15 us (8%)
  between operations  14.7 us (8%)
  matrix products  10.9 us (6%)
  local copies, waits for them, and re-layouts  6.22 us (3%)
  other arithmetic  2.26 us (1%)
    ppermute x28, starting transfers between devices, from_behind(): lax.ppermute(value, axis, [(source, source + steps) for source in range(l...  75.9 us
    unnamed x2, waiting for transfers between devices  33.7 us
    ppermute x28, waiting for transfers between devices, from_behind(): lax.ppermute(value, axis, [(source, source + steps) for source in range(l...  18.3 us
    all_gather x1, blocking collectives, shards(): shard_part = lax.all_gather(inputs, 'head', axis=1, tiled=True)  15 us
    unnamed x32, local copies, waits for them, and re-layouts  6.17 us
  transfers between devices with their start and end apart: 29, of which 5 were waited for; matrix products, arithmetic and copies ran while one was open for 5% of the time, Pallas kernels for 0%

commit v1 on v0

v1 whole, which is shorter than its diff:
```python
import functools
import math

import jax
import jax.numpy as jnp
from jax import lax
from jax.experimental import pallas as pl
from jax.experimental.pallas import tpu as pltpu
from jax.sharding import PartitionSpec as P

HEAD_DIM = 128
BLOCK = 128
DIMS_NT = (((1,), (1,)), ((), ()))
DIMS_TN = (((0,), (0,)), ((), ()))
DIMS_NN = (((1,), (0,)), ((), ()))
SCALE = 1.0 / math.sqrt(HEAD_DIM)
VMEM = pl.BlockSpec(memory_space=pltpu.VMEM)
SMEM = pl.BlockSpec(memory_space=pltpu.SMEM)


def dot(a, b, dims):
    return lax.dot_general(a, b, dims, preferred_element_type=jnp.float32)


def project_kernel(x_ref, wk_ref, wv_ref, bias_ref, kv_ref):
    rows = x_ref[...]
    keys = dot(rows, wk_ref[...], DIMS_NN)
    values = dot(rows, wv_ref[...], DIMS_NN) + bias_ref[...].astype(jnp.float32)
    kv_ref[:, :HEAD_DIM] = keys.astype(jnp.bfloat16)
    kv_ref[:, HEAD_DIM:] = values.astype(jnp.bfloat16)


def attention_kernel(
    place_ref, q_ref, c_ref, own_ref, sib_ref, r1_ref, r2_ref, r3_ref, sw_ref,
    att_ref, dq_ref, local_ref, near_ref, far_ref,
    keys, values, weights, dscores,
):
    place = place_ref[0]
    core = lax.rem(place, 2)
    group = q_ref.shape[1] // HEAD_DIM
    B = BLOCK
    first = jnp.where(core == 0, sw_ref[2 * B : 3 * B, :], sib_ref[...])
    parts = [own_ref[...], first, r1_ref[:B, :], r2_ref[:B, :], r3_ref[:B, :]]
    parts += [sw_ref[:B, :], sw_ref[B : 2 * B, :], sw_ref[3 * B :, :]]
    for slot, part in enumerate(parts):
        keys[slot * B : (slot + 1) * B, :] = part[:, :HEAD_DIM]
        values[slot * B : (slot + 1) * B, :] = part[:, HEAD_DIM:]
    near, far = jnp.int32(1) - core, core
    steps = [jnp.int32(1)]
    steps += [lax.shift_left(jnp.int32(1), bit + near) for bit in (5, 3, 1)]
    steps += [lax.shift_left(jnp.int32(1), bit + far) for bit in (5, 3, 1)]
    causal = lax.broadcasted_iota(jnp.int32, (B, B), 0) >= lax.broadcasted_iota(jnp.int32, (B, B), 1)
    penalty = [jnp.where(place >= step, 0.0, -jnp.inf).astype(jnp.float32) for step in steps]
    all_keys = keys[...]
    all_values = values[...]
    for head in range(group):
        cols = slice(head * HEAD_DIM, (head + 1) * HEAD_DIM)
        rows = slice(head * B, (head + 1) * B)
        query = q_ref[:, cols]
        grad = c_ref[:, cols]
        raw = dot(query, all_keys, DIMS_NT) * SCALE
        pieces = [jnp.where(causal, raw[:, :B], -jnp.inf)]
        for slot in range(1, 8):
            pieces.append(raw[:, slot * B : (slot + 1) * B] + penalty[slot - 1])
        scores = jnp.concatenate(pieces, axis=1)
        top = jnp.max(scores, axis=1, keepdims=True)
        raised = jnp.exp(scores - top)
        prob = raised * (1.0 / jnp.sum(raised, axis=1, keepdims=True))
        weight = prob.astype(jnp.bfloat16)
        weights[rows, :] = weight
        attended = dot(weight, all_values, DIMS_NN).astype(jnp.bfloat16)
        att_ref[:, cols] = attended
        delta = jnp.sum(
            grad.astype(jnp.float32) * attended.astype(jnp.float32), axis=1, keepdims=True
        )
        dprob = dot(grad, all_values, DIMS_NT)
        dscore = (prob * (dprob - delta)).astype(jnp.bfloat16)
        dscores[rows, :] = dscore
        dq_ref[:, cols] = (dot(dscore, all_keys, DIMS_NN) * SCALE).astype(jnp.bfloat16)
    queries = jnp.concatenate(
        [q_ref[:, h * HEAD_DIM : (h + 1) * HEAD_DIM] for h in range(group)], axis=0
    )
    grads = jnp.concatenate(
        [c_ref[:, h * HEAD_DIM : (h + 1) * HEAD_DIM] for h in range(group)], axis=0
    )
    for slot in range(8):
        cols = slice(slot * B, (slot + 1) * B)
        dkey = dot(dscores[:, cols], queries, DIMS_TN) * SCALE
        dvalue = dot(weights[:, cols], grads, DIMS_TN)
        if slot == 0:
            local_ref[:, :HEAD_DIM] = dkey
            local_ref[:, HEAD_DIM:] = dvalue
        else:
            target, row = (near_ref, slot - 2) if 2 <= slot < 5 else (far_ref, slot - 5)
            if slot == 1:
                target, row = far_ref, 3
            target[row * B : (row + 1) * B, :HEAD_DIM] = dkey.astype(jnp.bfloat16)
            target[row * B : (row + 1) * B, HEAD_DIM:] = dvalue.astype(jnp.bfloat16)


def finish_kernel(place_ref, local_ref, swap_ref, a1_ref, a2_ref, a3_ref, t_ref, wk_ref, wv_ref, out_ref):
    core = lax.rem(place_ref[0], 2)
    B = BLOCK
    total = local_ref[...]
    total += jnp.where(core == 0, swap_ref[3 * B :, :].astype(jnp.float32), 0.0)
    for ref in (a1_ref, a2_ref, a3_ref):
        total += ref[:B, :].astype(jnp.float32)
    total = (total + t_ref[...].astype(jnp.float32)).astype(jnp.bfloat16)
    width = wk_ref.shape[0] // 4
    for part in range(4):
        rows = slice(part * width, (part + 1) * width)
        term = dot(total[:, :HEAD_DIM], wk_ref[rows, :], DIMS_NT)
        term += dot(total[:, HEAD_DIM:], wv_ref[rows, :], DIMS_NT)
        out_ref[part * B : (part + 1) * B, :] = term.astype(jnp.bfloat16)


def add_kernel(parts_ref, out_ref):
    B = BLOCK
    total = parts_ref[:B, :].astype(jnp.float32)
    for part in range(1, 4):
        total += parts_ref[part * B : (part + 1) * B, :].astype(jnp.float32)
    out_ref[...] = total.astype(jnp.bfloat16)


def call(kernel, out_shape, args, scratch=(), flops=0):
    specs = [SMEM if a.dtype == jnp.int32 else VMEM for a in args]
    return pl.pallas_call(
        kernel,
        out_shape=out_shape,
        in_specs=specs,
        out_specs=jax.tree.map(lambda _: VMEM, out_shape),
        scratch_shapes=list(scratch),
        compiler_params=pltpu.CompilerParams(vmem_limit_bytes=30 * 1024 * 1024),
        cost_estimate=pl.CostEstimate(
            flops=flops,
            bytes_accessed=sum(a.size * a.dtype.itemsize for a in args),
            transcendentals=0,
        ),
    )(*args)


def swap(value, count):
    return lax.ppermute(value, "ctx", [(i, i ^ 1) for i in range(count)])


def shift(value, count, even, odd):
    pairs = []
    for i in range(count):
        to = i + (even if i % 2 == 0 else odd)
        if 0 <= to < count:
            pairs.append((i, to))
    return lax.ppermute(value, "ctx", pairs)


def shards(inputs, queries, w_key, w_value, v_bias, cotangent):
    count = lax.axis_size("ctx")
    place = lax.axis_index("ctx").astype(jnp.int32).reshape(1)
    B = BLOCK
    bf16 = jnp.bfloat16
    width = queries.shape[1]
    rows = lax.all_gather(inputs, "head", axis=1, tiled=True)
    own = call(
        project_kernel,
        jax.ShapeDtypeStruct((B, 2 * HEAD_DIM), bf16),
        (rows, w_key, w_value, v_bias.reshape(1, HEAD_DIM)),
        flops=4 * B * rows.shape[1] * HEAD_DIM,
    )
    sibling = swap(own, count)
    pair = jnp.concatenate([own, sibling], axis=0)
    r1 = shift(pair, count, 64, 32)
    r2 = shift(pair, count, 16, 8)
    r3 = shift(pair, count, 4, 2)
    swapped = swap(jnp.concatenate([r1[B:], r2[B:], r3], axis=0), count)
    attended, query_grad, local, near, far = call(
        attention_kernel,
        (
            jax.ShapeDtypeStruct((B, width), bf16),
            jax.ShapeDtypeStruct((B, width), bf16),
            jax.ShapeDtypeStruct((B, 2 * HEAD_DIM), jnp.float32),
            jax.ShapeDtypeStruct((3 * B, 2 * HEAD_DIM), bf16),
            jax.ShapeDtypeStruct((4 * B, 2 * HEAD_DIM), bf16),
        ),
        (place, queries, cotangent, own, sibling, r1, r2, r3, swapped),
        scratch=(
            pltpu.VMEM((8 * B, HEAD_DIM), bf16),
            pltpu.VMEM((8 * B, HEAD_DIM), bf16),
            pltpu.VMEM((width, 8 * B), bf16),
            pltpu.VMEM((width, 8 * B), bf16),
        ),
        flops=12 * width * 8 * B * HEAD_DIM,
    )
    back = swap(far, count)
    m1 = jnp.concatenate([near[:B], back[:B]], axis=0)
    m2 = jnp.concatenate([near[B : 2 * B], back[B : 2 * B]], axis=0)
    extra = jnp.where(place[0] % 2 == 1, back[3 * B :].astype(jnp.float32), 0.0)
    third = (near[2 * B :].astype(jnp.float32) + extra).astype(bf16)
    m3 = jnp.concatenate([third, back[2 * B : 3 * B]], axis=0)
    a1 = shift(m1, count, -64, -32)
    a2 = shift(m2, count, -16, -8)
    a3 = shift(m3, count, -4, -2)
    across = a1[B:].astype(jnp.float32) + a2[B:].astype(jnp.float32) + a3[B:].astype(jnp.float32)
    last = swap(across.astype(bf16), count)
    terms = call(
        finish_kernel,
        jax.ShapeDtypeStruct((4 * B, width), bf16),
        (place, local, back, a1, a2, a3, last, w_key, w_value),
        flops=4 * B * 4 * width * HEAD_DIM,
    )
    arrived = lax.all_to_all(terms, "head", 0, 0, tiled=True)
    input_grad = call(add_kernel, jax.ShapeDtypeStruct((B, width), bf16), (arrived,))
    return (attended, query_grad, input_grad)


def solution(mesh):
    return jax.shard_map(
        shards,
        mesh=mesh,
        in_specs=(
            P("ctx", "head"),
            P("ctx", "head"),
            P(None, "head"),
            P(None, "head"),
            P("head"),
            P("ctx", "head"),
        ),
        out_specs=(P("ctx", "head"), P("ctx", "head"), P("ctx", "head")),
        check_vma=False,
    )
```

time: 178 us -> 111 us (0.62)
  the two profiles are of different devices: /device:TPU:8 before, /device:TPU:56 now
where the time goes in v1:
time: 111 us
  starting transfers between devices  36.2 us (33%)
  blocking collectives  33 us (30%)
  waiting for transfers between devices  29.4 us (26%)
  Pallas kernels  8.43 us (8%)
  local copies, waits for them, and re-layouts  2.54 us (2%)
    ppermute x6, starting transfers between devices, shift(): return lax.ppermute(value, 'ctx', pairs)  28.4 us
    ppermute x6, waiting for transfers between devices, shift(): return lax.ppermute(value, 'ctx', pairs)  24.1 us
    all_to_all x1, blocking collectives, shards(): arrived = lax.all_to_all(terms, 'head', 0, 0, tiled=True)  18.1 us
    all_gather x1, blocking collectives, shards(): rows = lax.all_gather(inputs, 'head', axis=1, tiled=True)  15 us
    pallas_call x4, Pallas kernels, call(): pl.pallas_call(kernel, out_shape=out_shape, in_specs=specs, out_specs=jax...  8.43 us
    ppermute x4, starting transfers between devices, swap(): return lax.ppermute(value, 'ctx', [(i, i ^ 1) for i in range(count)])  7.8 us
    ppermute x4, waiting for transfers between devices, swap(): return lax.ppermute(value, 'ctx', [(i, i ^ 1) for i in range(count)])  5.28 us
    unnamed x16, local copies, waits for them, and re-layouts  2.51 us
  transfers between devices with their start and end apart: 10, of which 7 were waited for; matrix products, arithmetic and copies ran while one was open for 0% of the time, Pallas kernels for 0%

profile of v1, /device:TPU:56, one launch (start us, length us, event | category | flops | bytes accessed | tf_op | source)
XLA Modules:
  0.0 110.6 jit_solution(2142242421748344029)
XLA Ops:
  0.6 0.0 copy-start
  0.6 15.0 %all_gather.3.x_ref = bf16[128,3584]{1,0:T(8,128)(2,1)S(1)} all-gather(bf16[128,896]{1,0:T(8,128)(2,1)} %param.6), channel_id=1, replica_groups=mesh['ctx'=128,'head'=4] {'head'}, dimensions={1}, use_global_device_ids=true | all-gather | bytes 1146880 | tf_op jit(solution)/shard_map/all_gather | solution.py:161
  15.6 0.0 copy-start.5
  15.6 0.0 copy-done
  15.6 0.7 copy-done.5
  16.3 0.0 copy-start.1
  16.3 1.2 %copy-done.1 = bf16[3584,128]{1,0:T(8,128)(2,1)S(1)} copy-done((bf16[3584,128]{1,0:T(8,128)(2,1)S(1)}, bf16[3584,128]{1,0:T(8,128)(2,1)}, u32[]{:S(2)}) %copy-start.1) | copy-done | bytes 917528
  17.4 0.6 shard_map.85.own_ref
  18.1 1.9 %collective-permute-start = (bf16[128,256]{1,0:T(8,128)(2,1)S(1)}, bf16[128,256]{1,0:T(8,128)(2,1)S(1)}, u32[]{:S(2)}, u32[]{:S(2)}) collective-permute-start(bf16[128,256]{1,0:T(8,128)(2,1)S(1)} %shard_map.85.own_ref), channel_id=1, source_target_pairs={{0,4},{4,0},{8,12},{12,8},{16,20},{20,16},{24,28},{28,24},{32,36},... | collective-permute-start | bytes 196616 | tf_op jit(solution)/shard_map/ppermute | solution.py:143
  20.0 1.2 %collective-permute-done.sib_ref = bf16[128,256]{1,0:T(8,128)(2,1)S(1)} collective-permute-done((bf16[128,256]{1,0:T(8,128)(2,1)S(1)}, bf16[128,256]{1,0:T(8,128)(2,1)S(1)}, u32[]{:S(2)}, u32[]{:S(2)}) %collective-permute-start) | collective-permute-done | bytes 65568 | tf_op jit(solution)/shard_map/ppermute | solution.py:143
  21.2 5.2 %collective-permute-start.2 = (bf16[256,256]{1,0:T(8,128)(2,1)S(1)}, bf16[256,256]{1,0:T(8,128)(2,1)S(1)}, u32[]{:S(2)}, u32[]{:S(2)}) collective-permute-start(bf16[256,256]{1,0:T(8,128)(2,1)S(1)} %pad_maximum_fusion.1), channel_id=1, source_target_pairs={{0,64},{4,36},{8,72},{12,44},{16,80},{20,52},{24,88},{28,60},{32,9... | collective-permute-start | bytes 393224 | tf_op jit(solution)/shard_map/ppermute | solution.py:152
  26.4 13.0 %collective-permute-start.1 = (bf16[256,256]{1,0:T(8,128)(2,1)S(1)}, bf16[256,256]{1,0:T(8,128)(2,1)S(1)}, u32[]{:S(2)}, u32[]{:S(2)}) collective-permute-start(bf16[256,256]{1,0:T(8,128)(2,1)S(1)} %pad_maximum_fusion.1), channel_id=1, source_target_pairs={{0,256},{4,132},{8,264},{12,140},{16,272},{20,148},{24,280},{28,15... | collective-permute-start | bytes 393224 | tf_op jit(solution)/shard_map/ppermute | solution.py:152
  39.5 3.6 %collective-permute-start.3 = (bf16[256,256]{1,0:T(8,128)(2,1)S(1)}, bf16[256,256]{1,0:T(8,128)(2,1)S(1)}, u32[]{:S(2)}, u32[]{:S(2)}) collective-permute-start(bf16[256,256]{1,0:T(8,128)(2,1)S(1)} %pad_maximum_fusion.1), channel_id=1, source_target_pairs={{0,16},{4,12},{8,24},{12,20},{16,32},{20,28},{24,40},{28,36},{32,4... | collective-permute-start | bytes 393224 | tf_op jit(solution)/shard_map/ppermute | solution.py:152
  43.1 0.0 collective-permute-done.2.r2_ref
  43.1 0.0 copy-start.3
  43.1 0.6 copy-done.3
  43.7 2.4 %collective-permute-done.1.r1_ref = bf16[256,256]{1,0:T(8,128)(2,1)S(1)} collective-permute-done((bf16[256,256]{1,0:T(8,128)(2,1)S(1)}, bf16[256,256]{1,0:T(8,128)(2,1)S(1)}, u32[]{:S(2)}, u32[]{:S(2)}) %collective-permute-start.1) | collective-permute-done | bytes 131104 | tf_op jit(solution)/shard_map/ppermute | solution.py:152
  46.1 0.0 slice-start
  46.1 0.0 copy-start.7
  46.1 0.0 copy-start.4
  46.2 0.0 copy-start.6
  46.2 1.7 %collective-permute-done.3.r3_ref = bf16[256,256]{1,0:T(8,128)(2,1)S(1)} collective-permute-done((bf16[256,256]{1,0:T(8,128)(2,1)S(1)}, bf16[256,256]{1,0:T(8,128)(2,1)S(1)}, u32[]{:S(2)}, u32[]{:S(2)}) %collective-permute-start.3) | collective-permute-done | bytes 131104 | tf_op jit(solution)/shard_map/ppermute | solution.py:152
  47.8 0.0 slice-done
  47.8 1.9 %collective-permute-start.4 = (bf16[512,256]{1,0:T(8,128)(2,1)S(1)}, bf16[512,256]{1,0:T(8,128)(2,1)S(1)}, u32[]{:S(2)}, u32[]{:S(2)}) collective-permute-start(bf16[512,256]{1,0:T(8,128)(2,1)S(1)} %pad_maximum_fusion), channel_id=1, source_target_pairs={{0,4},{4,0},{8,12},{12,8},{16,20},{20,16},{24,28},{28,24},{32,36},... | collective-permute-start | bytes 786440 | tf_op jit(solution)/shard_map/ppermute | solution.py:143
  49.8 1.5 %collective-permute-done.4.sw_ref = bf16[512,256]{1,0:T(8,128)(2,1)S(1)} collective-permute-done((bf16[512,256]{1,0:T(8,128)(2,1)S(1)}, bf16[512,256]{1,0:T(8,128)(2,1)S(1)}, u32[]{:S(2)}, u32[]{:S(2)}) %collective-permute-start.4) | collective-permute-done | bytes 262176 | tf_op jit(solution)/shard_map/ppermute | solution.py:143
  51.3 0.0 copy-done.7
  51.3 0.0 copy-done.4
  51.3 0.0 copy-done.6
  51.3 6.3 %shard_map.86 = (bf16[128,896]{1,0:T(8,128)(2,1)}, bf16[128,896]{1,0:T(8,128)(2,1)}, f32[128,256]{1,0:T(8,128)S(1)}, bf16[384,256]{1,0:T(8,128)(2,1)S(1)}, bf16[512,256]{1,0:T(8,128)(2,1)S(1)}) custom-call(s32[1]{0:T(128)} %bitcast.place_ref, bf16[128,896]{1,0:T(8,128)(2,1)S(1)} %copy-done.6, bf16[128,896]{1,0:T(8,128)(2,1)S(1)} %copy-done.7, ...), custom_call_target="tpu_custom_call" | custom-call | flops 1409286144 | bytes 1245188 | tf_op jit(solution)/shard_map/pallas_call | solution.py:127
  57.6 2.0 %collective-permute-start.5 = (bf16[512,256]{1,0:T(8,128)(2,1)S(1)}, bf16[512,256]{1,0:T(8,128)(2,1)S(1)}, u32[]{:S(2)}, u32[]{:S(2)}) collective-permute-start(bf16[512,256]{1,0:T(8,128)(2,1)S(1)} %get-tuple-element.11), channel_id=1, source_target_pairs={{0,4},{4,0},{8,12},{12,8},{16,20},{20,16},{24,28},{28,24},{32,36},... | collective-permute-start | bytes 786440 | tf_op jit(solution)/shard_map/ppermute | solution.py:143
  59.6 0.0 copy-start.2
  59.6 1.3 %collective-permute-done.5.swap_ref = bf16[512,256]{1,0:T(8,128)(2,1)S(1)} collective-permute-done((bf16[512,256]{1,0:T(8,128)(2,1)S(1)}, bf16[512,256]{1,0:T(8,128)(2,1)S(1)}, u32[]{:S(2)}, u32[]{:S(2)}) %collective-permute-start.5) | collective-permute-done | bytes 262176 | tf_op jit(solution)/shard_map/ppermute | solution.py:143
  61.0 1.3 %collective-permute-start.6 = (bf16[256,256]{1,0:T(8,128)(2,1)S(1)}, bf16[256,256]{1,0:T(8,128)(2,1)S(1)}, u32[]{:S(2)}, u32[]{:S(2)}) collective-permute-start(bf16[256,256]{1,0:T(8,128)(2,1)S(1)} %pad_maximum_fusion.2), channel_id=1, source_target_pairs={{132,4},{140,12},{148,20},{156,28},{164,36},{172,44},{180,52},{188... | collective-permute-start | bytes 393224 | tf_op jit(solution)/shard_map/ppermute | solution.py:152
  62.3 1.3 %collective-permute-start.7 = (bf16[256,256]{1,0:T(8,128)(2,1)S(1)}, bf16[256,256]{1,0:T(8,128)(2,1)S(1)}, u32[]{:S(2)}, u32[]{:S(2)}) collective-permute-start(bf16[256,256]{1,0:T(8,128)(2,1)S(1)} %pad_maximum_fusion.3), channel_id=1, source_target_pairs={{36,4},{44,12},{52,20},{60,28},{64,0},{68,36},{72,8},{76,44},{80,1... | collective-permute-start | bytes 393224 | tf_op jit(solution)/shard_map/ppermute | solution.py:152
  63.7 4.0 %collective-permute-start.8 = (bf16[256,256]{1,0:T(8,128)(2,1)S(1)}, bf16[256,256]{1,0:T(8,128)(2,1)S(1)}, u32[]{:S(2)}, u32[]{:S(2)}) collective-permute-start(bf16[256,256]{1,0:T(8,128)(2,1)S(1)} %pad_maximum_fusion.4), channel_id=1, source_target_pairs={{12,4},{16,0},{20,12},{24,8},{28,20},{32,16},{36,28},{40,24},{44,3... | collective-permute-start | bytes 393224 | tf_op jit(solution)/shard_map/ppermute | solution.py:152
  67.7 20.1 %collective-permute-done.6.a1_ref = bf16[256,256]{1,0:T(8,128)(2,1)S(1)} collective-permute-done((bf16[256,256]{1,0:T(8,128)(2,1)S(1)}, bf16[256,256]{1,0:T(8,128)(2,1)S(1)}, u32[]{:S(2)}, u32[]{:S(2)}) %collective-permute-start.6) | collective-permute-done | bytes 131104 | tf_op jit(solution)/shard_map/ppermute | solution.py:152
  87.8 0.0 collective-permute-done.7.a2_ref
  87.8 0.0 collective-permute-done.8.a3_ref
  87.9 1.9 %collective-permute-start.9 = (bf16[128,256]{1,0:T(8,128)(2,1)S(1)}, bf16[128,256]{1,0:T(8,128)(2,1)S(1)}, u32[]{:S(2)}, u32[]{:S(2)}) collective-permute-start(bf16[128,256]{1,0:T(8,128)(2,1)S(1)} %add_convert_fusion), channel_id=1, source_target_pairs={{0,4},{4,0},{8,12},{12,8},{16,20},{20,16},{24,28},{28,24},{32,36},... | collective-permute-start | bytes 196616 | tf_op jit(solution)/shard_map/ppermute | solution.py:143
  89.8 1.2 %collective-permute-done.9.t_ref = bf16[128,256]{1,0:T(8,128)(2,1)S(1)} collective-permute-done((bf16[128,256]{1,0:T(8,128)(2,1)S(1)}, bf16[128,256]{1,0:T(8,128)(2,1)S(1)}, u32[]{:S(2)}, u32[]{:S(2)}) %collective-permute-start.9) | collective-permute-done | bytes 65568 | tf_op jit(solution)/shard_map/ppermute | solution.py:143
  91.0 0.0 copy-done.2
  91.0 0.7 shard_map.87
  91.7 18.1 %all_to_all.11 = bf16[4,128,896]{2,1,0:T(8,128)(2,1)S(1)} all-to-all(bf16[4,128,896]{2,1,0:T(8,128)(2,1)S(1)} %bitcast.5), channel_id=1, replica_groups=mesh['ctx'=128,'head'=4] {'head'}, dimensions={0} | all-to-all | bytes 1835008 | tf_op jit(solution)/shard_map/all_to_all | solution.py:209
  109.8 0.8 shard_map.88
  (10 shorter events, 0.1 us)
Async XLA Ops:
  0.6 15.0 %copy-start = (bf16[3584,128]{1,0:T(8,128)(2,1)S(1)}, bf16[3584,128]{1,0:T(8,128)(2,1)}, u32[]{:S(2)}) copy-start(bf16[3584,128]{1,0:T(8,128)(2,1)} %wk_ref.3) | copy-start | bytes 2752516
  15.6 0.7 copy-start.5
  16.3 1.2 %copy-start.1 = (bf16[3584,128]{1,0:T(8,128)(2,1)S(1)}, bf16[3584,128]{1,0:T(8,128)(2,1)}, u32[]{:S(2)}) copy-start(bf16[3584,128]{1,0:T(8,128)(2,1)} %wv_ref.3) | copy-start | bytes 2752516
  18.1 3.1 %collective-permute-start = (bf16[128,256]{1,0:T(8,128)(2,1)S(1)}, bf16[128,256]{1,0:T(8,128)(2,1)S(1)}, u32[]{:S(2)}, u32[]{:S(2)}) collective-permute-start(bf16[128,256]{1,0:T(8,128)(2,1)S(1)} %shard_map.85.own_ref), channel_id=1, source_target_pairs={{0,4},{4,0},{8,12},{12,8},{16,20},{20,16},{24,28},{28,24},{32,36},... | collective-permute-start | bytes 196616 | tf_op jit(solution)/shard_map/ppermute | solution.py:143
  21.2 21.8 %collective-permute-start.2 = (bf16[256,256]{1,0:T(8,128)(2,1)S(1)}, bf16[256,256]{1,0:T(8,128)(2,1)S(1)}, u32[]{:S(2)}, u32[]{:S(2)}) collective-permute-start(bf16[256,256]{1,0:T(8,128)(2,1)S(1)} %pad_maximum_fusion.1), channel_id=1, source_target_pairs={{0,64},{4,36},{8,72},{12,44},{16,80},{20,52},{24,88},{28,60},{32,9... | collective-permute-start | bytes 393224 | tf_op jit(solution)/shard_map/ppermute | solution.py:152
  26.4 19.7 %collective-permute-start.1 = (bf16[256,256]{1,0:T(8,128)(2,1)S(1)}, bf16[256,256]{1,0:T(8,128)(2,1)S(1)}, u32[]{:S(2)}, u32[]{:S(2)}) collective-permute-start(bf16[256,256]{1,0:T(8,128)(2,1)S(1)} %pad_maximum_fusion.1), channel_id=1, source_target_pairs={{0,256},{4,132},{8,264},{12,140},{16,272},{20,148},{24,280},{28,15... | collective-permute-start | bytes 393224 | tf_op jit(solution)/shard_map/ppermute | solution.py:152
  39.5 8.4 %collective-permute-start.3 = (bf16[256,256]{1,0:T(8,128)(2,1)S(1)}, bf16[256,256]{1,0:T(8,128)(2,1)S(1)}, u32[]{:S(2)}, u32[]{:S(2)}) collective-permute-start(bf16[256,256]{1,0:T(8,128)(2,1)S(1)} %pad_maximum_fusion.1), channel_id=1, source_target_pairs={{0,16},{4,12},{8,24},{12,20},{16,32},{20,28},{24,40},{28,36},{32,4... | collective-permute-start | bytes 393224 | tf_op jit(solution)/shard_map/ppermute | solution.py:152
  43.1 0.7 copy-start.3
  46.1 1.7 %slice-start = ((bf16[256,256]{1,0:T(8,128)(2,1)}), bf16[128,256]{1,0:T(8,128)(2,1)S(1)}, s32[]{:S(2)}) async-start(bf16[256,256]{1,0:T(8,128)(2,1)} %copy-done.3), calls=%async_computation.1 | async-start | bytes 131072 | tf_op jit(solution)/shard_map/slice | solution.py:173
  46.1 5.1 %copy-start.7 = (bf16[128,896]{1,0:T(8,128)(2,1)S(1)}, bf16[128,896]{1,0:T(8,128)(2,1)}, u32[]{:S(2)}) copy-start(bf16[128,896]{1,0:T(8,128)(2,1)} %c_ref.1) | copy-start | bytes 688132
  46.1 5.1 %copy-start.4 = (bf16[256,256]{1,0:T(8,128)(2,1)S(1)}, bf16[256,256]{1,0:T(8,128)(2,1)}, u32[]{:S(2)}) copy-start(bf16[256,256]{1,0:T(8,128)(2,1)} %copy-done.3) | copy-start | bytes 393220
  46.2 5.1 %copy-start.6 = (bf16[128,896]{1,0:T(8,128)(2,1)S(1)}, bf16[128,896]{1,0:T(8,128)(2,1)}, u32[]{:S(2)}) copy-start(bf16[128,896]{1,0:T(8,128)(2,1)} %q_ref.1) | copy-start | bytes 688132
  47.8 3.4 %collective-permute-start.4 = (bf16[512,256]{1,0:T(8,128)(2,1)S(1)}, bf16[512,256]{1,0:T(8,128)(2,1)S(1)}, u32[]{:S(2)}, u32[]{:S(2)}) collective-permute-start(bf16[512,256]{1,0:T(8,128)(2,1)S(1)} %pad_maximum_fusion), channel_id=1, source_target_pairs={{0,4},{4,0},{8,12},{12,8},{16,20},{20,16},{24,28},{28,24},{32,36},... | collective-permute-start | bytes 786440 | tf_op jit(solution)/shard_map/ppermute | solution.py:143
  57.6 3.4 %collective-permute-start.5 = (bf16[512,256]{1,0:T(8,128)(2,1)S(1)}, bf16[512,256]{1,0:T(8,128)(2,1)S(1)}, u32[]{:S(2)}, u32[]{:S(2)}) collective-permute-start(bf16[512,256]{1,0:T(8,128)(2,1)S(1)} %get-tuple-element.11), channel_id=1, source_target_pairs={{0,4},{4,0},{8,12},{12,8},{16,20},{20,16},{24,28},{28,24},{32,36},... | collective-permute-start | bytes 786440 | tf_op jit(solution)/shard_map/ppermute | solution.py:143
  59.6 31.4 %copy-start.2 = (bf16[3584,128]{1,0:T(8,128)(2,1)S(1)}, bf16[3584,128]{1,0:T(8,128)(2,1)}, u32[]{:S(2)}) copy-start(bf16[3584,128]{1,0:T(8,128)(2,1)} %wv_ref.3) | copy-start | bytes 2752516
  61.0 26.8 %collective-permute-start.6 = (bf16[256,256]{1,0:T(8,128)(2,1)S(1)}, bf16[256,256]{1,0:T(8,128)(2,1)S(1)}, u32[]{:S(2)}, u32[]{:S(2)}) collective-permute-start(bf16[256,256]{1,0:T(8,128)(2,1)S(1)} %pad_maximum_fusion.2), channel_id=1, source_target_pairs={{132,4},{140,12},{148,20},{156,28},{164,36},{172,44},{180,52},{188... | collective-permute-start | bytes 393224 | tf_op jit(solution)/shard_map/ppermute | solution.py:152
  62.3 25.5 %collective-permute-start.7 = (bf16[256,256]{1,0:T(8,128)(2,1)S(1)}, bf16[256,256]{1,0:T(8,128)(2,1)S(1)}, u32[]{:S(2)}, u32[]{:S(2)}) collective-permute-start(bf16[256,256]{1,0:T(8,128)(2,1)S(1)} %pad_maximum_fusion.3), channel_id=1, source_target_pairs={{36,4},{44,12},{52,20},{60,28},{64,0},{68,36},{72,8},{76,44},{80,1... | collective-permute-start | bytes 393224 | tf_op jit(solution)/shard_map/ppermute | solution.py:152
  63.7 24.1 %collective-permute-start.8 = (bf16[256,256]{1,0:T(8,128)(2,1)S(1)}, bf16[256,256]{1,0:T(8,128)(2,1)S(1)}, u32[]{:S(2)}, u32[]{:S(2)}) collective-permute-start(bf16[256,256]{1,0:T(8,128)(2,1)S(1)} %pad_maximum_fusion.4), channel_id=1, source_target_pairs={{12,4},{16,0},{20,12},{24,8},{28,20},{32,16},{36,28},{40,24},{44,3... | collective-permute-start | bytes 393224 | tf_op jit(solution)/shard_map/ppermute | solution.py:152
  87.9 3.1 %collective-permute-start.9 = (bf16[128,256]{1,0:T(8,128)(2,1)S(1)}, bf16[128,256]{1,0:T(8,128)(2,1)S(1)}, u32[]{:S(2)}, u32[]{:S(2)}) collective-permute-start(bf16[128,256]{1,0:T(8,128)(2,1)S(1)} %add_convert_fusion), channel_id=1, source_target_pairs={{0,4},{4,0},{8,12},{12,8},{16,20},{20,16},{24,28},{28,24},{32,36},... | collective-permute-start | bytes 196616 | tf_op jit(solution)/shard_map/ppermute | solution.py:143

commit v2 on v1

--- a/solution.py
+++ b/solution.py
@@ -22,12 +22,32 @@
     return lax.dot_general(a, b, dims, preferred_element_type=jnp.float32)
 
 
-def project_kernel(x_ref, wk_ref, wv_ref, bias_ref, kv_ref):
+def project_kernel(x_ref, wk_hbm, wv_hbm, bias_hbm, kv_ref, wk, wv, bias, sems):
+    pairs = [(wk_hbm, wk), (bias_hbm, bias), (wv_hbm, wv)]
+    copies = [pltpu.make_async_copy(a, b, sems.at[i]) for i, (a, b) in enumerate(pairs)]
+    for copy in copies:
+        copy.start()
     rows = x_ref[...]
-    keys = dot(rows, wk_ref[...], DIMS_NN)
-    values = dot(rows, wv_ref[...], DIMS_NN) + bias_ref[...].astype(jnp.float32)
-    kv_ref[:, :HEAD_DIM] = keys.astype(jnp.bfloat16)
+    copies[0].wait()
+    kv_ref[:, :HEAD_DIM] = dot(rows, wk[...], DIMS_NN).astype(jnp.bfloat16)
+    copies[1].wait()
+    copies[2].wait()
+    values = dot(rows, wv[...], DIMS_NN) + bias[...].astype(jnp.float32)
     kv_ref[:, HEAD_DIM:] = values.astype(jnp.bfloat16)
+
+
+def half_kernel(r1_ref, out_ref):
+    out_ref[...] = r1_ref[BLOCK:, :]
+
+
+def join_kernel(s1_ref, r2_ref, out_ref):
+    out_ref[:BLOCK, :] = s1_ref[...]
+    out_ref[BLOCK:, :] = r2_ref[BLOCK:, :]
+
+
+def pack_kernel(s12_ref, r3_ref, out_ref):
+    out_ref[: 2 * BLOCK, :] = s12_ref[...]
+    out_ref[2 * BLOCK :, :] = r3_ref[...]
 
 
 def attention_kernel(
@@ -122,13 +142,23 @@
     out_ref[...] = total.astype(jnp.bfloat16)
 
 
-def call(kernel, out_shape, args, scratch=(), flops=0):
+def out_spec(shape):
+    return VMEM if isinstance(shape, jax.ShapeDtypeStruct) else pl.BlockSpec(memory_space=pltpu.HBM)
+
+
+def call(kernel, out_shape, args, scratch=(), flops=0, hbm=()):
     specs = [SMEM if a.dtype == jnp.int32 else VMEM for a in args]
+    for index in hbm:
+        specs[index] = pl.BlockSpec(memory_space=pltpu.HBM)
+    args = [
+        pltpu.with_memory_space_constraint(a, pltpu.HBM) if i in hbm else a
+        for i, a in enumerate(args)
+    ]
     return pl.pallas_call(
         kernel,
         out_shape=out_shape,
         in_specs=specs,
-        out_specs=jax.tree.map(lambda _: VMEM, out_shape),
+        out_specs=jax.tree.map(out_spec, out_shape),
         scratch_shapes=list(scratch),
         compiler_params=pltpu.CompilerParams(vmem_limit_bytes=30 * 1024 * 1024),
         cost_estimate=pl.CostEstimate(
@@ -163,14 +193,24 @@
         project_kernel,
         jax.ShapeDtypeStruct((B, 2 * HEAD_DIM), bf16),
         (rows, w_key, w_value, v_bias.reshape(1, HEAD_DIM)),
+        scratch=(
+            pltpu.VMEM(w_key.shape, bf16),
+            pltpu.VMEM(w_value.shape, bf16),
+            pltpu.VMEM((1, HEAD_DIM), bf16),
+            pltpu.SemaphoreType.DMA((3,)),
+        ),
         flops=4 * B * rows.shape[1] * HEAD_DIM,
+        hbm=(1, 2, 3),
     )
     sibling = swap(own, count)
     pair = jnp.concatenate([own, sibling], axis=0)
     r1 = shift(pair, count, 64, 32)
     r2 = shift(pair, count, 16, 8)
     r3 = shift(pair, count, 4, 2)
-    swapped = swap(jnp.concatenate([r1[B:], r2[B:], r3], axis=0), count)
+    packed = call(half_kernel, jax.ShapeDtypeStruct((B, 2 * HEAD_DIM), bf16), (r1,))
+    packed = call(join_kernel, jax.ShapeDtypeStruct((2 * B, 2 * HEAD_DIM), bf16), (packed, r2))
+    packed = call(pack_kernel, jax.ShapeDtypeStruct((4 * B, 2 * HEAD_DIM), bf16), (packed, r3))
+    swapped = swap(packed, count)
     attended, query_grad, local, near, far = call(
         attention_kernel,
         (

time: 111 us -> 108 us (0.973)
  local copies, waits for them, and re-layouts: 2.54 us -> 0.05 us
  Pallas kernels: 8.43 us -> 9.82 us
  waiting for transfers between devices: 29.4 us -> 28.1 us
    unnamed x16 -> x8, local copies, waits for them, and re-layouts: 2.51 us -> 0.03 us
    pallas_call x4 -> x7, Pallas kernels: 8.43 us -> 9.82 us  [call(): pl.pallas_call(kernel, out_shape=out_shape, in_specs=specs, out_specs=jax...]
    ppermute x6, waiting for transfers between devices: 24.1 us -> 22.9 us  [shift(): return lax.ppermute(value, 'ctx', pairs)]
where the time goes in v2:
time: 108 us
  starting transfers between devices  36.2 us (34%)
  blocking collectives  32.9 us (30%)
  waiting for transfers between devices  28.1 us (26%)
  Pallas kernels  9.82 us (9%)
    ppermute x6, starting transfers between devices, shift(): return lax.ppermute(value, 'ctx', pairs)  28.4 us
    ppermute x6, waiting for transfers between devices, shift(): return lax.ppermute(value, 'ctx', pairs)  22.9 us
    all_to_all x1, blocking collectives, shards(): arrived = lax.all_to_all(terms, 'head', 0, 0, tiled=True)  18 us
    all_gather x1, blocking collectives, shards(): rows = lax.all_gather(inputs, 'head', axis=1, tiled=True)  14.8 us
    pallas_call x7, Pallas kernels, call(): pl.pallas_call(kernel, out_shape=out_shape, in_specs=specs, out_specs=jax...  9.82 us
    ppermute x4, starting transfers between devices, swap(): return lax.ppermute(value, 'ctx', [(i, i ^ 1) for i in range(count)])  7.81 us
    ppermute x4, waiting for transfers between devices, swap(): return lax.ppermute(value, 'ctx', [(i, i ^ 1) for i in range(count)])  5.26 us
  transfers between devices with their start and end apart: 10, of which 7 were waited for; matrix products, arithmetic and copies ran while one was open for 0% of the time, Pallas kernels for 0%

profile of v2, /device:TPU:56, one launch (start us, length us, event | category | flops | bytes accessed | tf_op | source)
XLA Modules:
  0.0 108.1 jit_solution(17543616022461103649)
XLA Ops:
  0.6 14.8 %all_gather.3.x_ref = bf16[128,3584]{1,0:T(8,128)(2,1)S(1)} all-gather(bf16[128,896]{1,0:T(8,128)(2,1)} %param.6), channel_id=1, replica_groups=mesh['ctx'=128,'head'=4] {'head'}, dimensions={1}, use_global_device_ids=true | all-gather | bytes 1146880 | tf_op jit(solution)/shard_map/all_gather | solution.py:191
  15.5 2.0 %shard_map.85.own_ref = bf16[128,256]{1,0:T(8,128)(2,1)S(1)} custom-call(bf16[128,3584]{1,0:T(8,128)(2,1)S(1)} %all_gather.3.x_ref, bf16[3584,128]{1,0:T(8,128)(2,1)} %wk_ref.1, bf16[3584,128]{1,0:T(8,128)(2,1)} %wv_ref.1, bf16[1,128]{1,0:T(2,128)(2,1)} %bitcast.6), custom_call_target="tpu_custom_call" | custom-call | flops 234881024 | bytes 2752768 | tf_op jit(solution)/shard_map/pallas_call | solution.py:157
  17.5 1.9 %collective-permute-start = (bf16[128,256]{1,0:T(8,128)(2,1)S(1)}, bf16[128,256]{1,0:T(8,128)(2,1)S(1)}, u32[]{:S(2)}, u32[]{:S(2)}) collective-permute-start(bf16[128,256]{1,0:T(8,128)(2,1)S(1)} %shard_map.85.own_ref), channel_id=1, source_target_pairs={{0,4},{4,0},{8,12},{12,8},{16,20},{20,16},{24,28},{28,24},{32,36},... | collective-permute-start | bytes 196616 | tf_op jit(solution)/shard_map/ppermute | solution.py:173
  19.4 1.2 %collective-permute-done.sib_ref = bf16[128,256]{1,0:T(8,128)(2,1)S(1)} collective-permute-done((bf16[128,256]{1,0:T(8,128)(2,1)S(1)}, bf16[128,256]{1,0:T(8,128)(2,1)S(1)}, u32[]{:S(2)}, u32[]{:S(2)}) %collective-permute-start) | collective-permute-done | bytes 65568 | tf_op jit(solution)/shard_map/ppermute | solution.py:173
  20.6 14.8 %collective-permute-start.1 = (bf16[256,256]{1,0:T(8,128)(2,1)S(1)}, bf16[256,256]{1,0:T(8,128)(2,1)S(1)}, u32[]{:S(2)}, u32[]{:S(2)}) collective-permute-start(bf16[256,256]{1,0:T(8,128)(2,1)S(1)} %pad_maximum_fusion), channel_id=1, source_target_pairs={{0,256},{4,132},{8,264},{12,140},{16,272},{20,148},{24,280},{28,15... | collective-permute-start | bytes 393224 | tf_op jit(solution)/shard_map/ppermute | solution.py:182
  35.5 3.4 %collective-permute-start.2 = (bf16[256,256]{1,0:T(8,128)(2,1)S(1)}, bf16[256,256]{1,0:T(8,128)(2,1)S(1)}, u32[]{:S(2)}, u32[]{:S(2)}) collective-permute-start(bf16[256,256]{1,0:T(8,128)(2,1)S(1)} %pad_maximum_fusion), channel_id=1, source_target_pairs={{0,64},{4,36},{8,72},{12,44},{16,80},{20,52},{24,88},{28,60},{32,9... | collective-permute-start | bytes 393224 | tf_op jit(solution)/shard_map/ppermute | solution.py:182
  38.8 3.6 %collective-permute-start.3 = (bf16[256,256]{1,0:T(8,128)(2,1)S(1)}, bf16[256,256]{1,0:T(8,128)(2,1)S(1)}, u32[]{:S(2)}, u32[]{:S(2)}) collective-permute-start(bf16[256,256]{1,0:T(8,128)(2,1)S(1)} %pad_maximum_fusion), channel_id=1, source_target_pairs={{0,16},{4,12},{8,24},{12,20},{16,32},{20,28},{24,40},{28,36},{32,4... | collective-permute-start | bytes 393224 | tf_op jit(solution)/shard_map/ppermute | solution.py:182
  42.4 0.0 collective-permute-done.1.r1_ref
  42.5 0.2 collective-permute-done.2.r2_ref
  42.7 0.0 copy-start.2
  42.7 0.0 copy-start.3
  42.7 4.5 %collective-permute-done.3.r3_ref = bf16[256,256]{1,0:T(8,128)(2,1)S(1)} collective-permute-done((bf16[256,256]{1,0:T(8,128)(2,1)S(1)}, bf16[256,256]{1,0:T(8,128)(2,1)S(1)}, u32[]{:S(2)}, u32[]{:S(2)}) %collective-permute-start.3) | collective-permute-done | bytes 131104 | tf_op jit(solution)/shard_map/ppermute | solution.py:182
  47.2 1.9 %collective-permute-start.4 = (bf16[512,256]{1,0:T(8,128)(2,1)S(1)}, bf16[512,256]{1,0:T(8,128)(2,1)S(1)}, u32[]{:S(2)}, u32[]{:S(2)}) collective-permute-start(bf16[512,256]{1,0:T(8,128)(2,1)S(1)} %shard_map.88), channel_id=1, source_target_pairs={{0,4},{4,0},{8,12},{12,8},{16,20},{20,16},{24,28},{28,24},{32,36},... | collective-permute-start | bytes 786440 | tf_op jit(solution)/shard_map/ppermute | solution.py:173
  49.2 1.5 %collective-permute-done.4.sw_ref = bf16[512,256]{1,0:T(8,128)(2,1)S(1)} collective-permute-done((bf16[512,256]{1,0:T(8,128)(2,1)S(1)}, bf16[512,256]{1,0:T(8,128)(2,1)S(1)}, u32[]{:S(2)}, u32[]{:S(2)}) %collective-permute-start.4) | collective-permute-done | bytes 262176 | tf_op jit(solution)/shard_map/ppermute | solution.py:173
  50.7 0.0 copy-done.2
  50.7 0.0 copy-done.3
  50.7 6.3 %shard_map.89 = (bf16[128,896]{1,0:T(8,128)(2,1)}, bf16[128,896]{1,0:T(8,128)(2,1)}, f32[128,256]{1,0:T(8,128)S(1)}, bf16[384,256]{1,0:T(8,128)(2,1)S(1)}, bf16[512,256]{1,0:T(8,128)(2,1)S(1)}) custom-call(s32[1]{0:T(128)} %bitcast.place_ref, bf16[128,896]{1,0:T(8,128)(2,1)S(1)} %copy-done.2, bf16[128,896]{1,0:T(8,128)(2,1)S(1)} %copy-done.3, ...), custom_call_target="tpu_custom_call" | custom-call | flops 1409286144 | bytes 1245188 | tf_op jit(solution)/shard_map/pallas_call | solution.py:157
  56.9 2.0 %collective-permute-start.5 = (bf16[512,256]{1,0:T(8,128)(2,1)S(1)}, bf16[512,256]{1,0:T(8,128)(2,1)S(1)}, u32[]{:S(2)}, u32[]{:S(2)}) collective-permute-start(bf16[512,256]{1,0:T(8,128)(2,1)S(1)} %get-tuple-element.11), channel_id=1, source_target_pairs={{0,4},{4,0},{8,12},{12,8},{16,20},{20,16},{24,28},{28,24},{32,36},... | collective-permute-start | bytes 786440 | tf_op jit(solution)/shard_map/ppermute | solution.py:173
  59.0 0.0 copy-start
  59.0 0.0 copy-start.1
  59.0 1.3 %collective-permute-done.5.swap_ref = bf16[512,256]{1,0:T(8,128)(2,1)S(1)} collective-permute-done((bf16[512,256]{1,0:T(8,128)(2,1)S(1)}, bf16[512,256]{1,0:T(8,128)(2,1)S(1)}, u32[]{:S(2)}, u32[]{:S(2)}) %collective-permute-start.5) | collective-permute-done | bytes 262176 | tf_op jit(solution)/shard_map/ppermute | solution.py:173
  60.4 1.3 %collective-permute-start.6 = (bf16[256,256]{1,0:T(8,128)(2,1)S(1)}, bf16[256,256]{1,0:T(8,128)(2,1)S(1)}, u32[]{:S(2)}, u32[]{:S(2)}) collective-permute-start(bf16[256,256]{1,0:T(8,128)(2,1)S(1)} %pad_maximum_fusion.1), channel_id=1, source_target_pairs={{132,4},{140,12},{148,20},{156,28},{164,36},{172,44},{180,52},{188... | collective-permute-start | bytes 393224 | tf_op jit(solution)/shard_map/ppermute | solution.py:182
  61.7 1.3 %collective-permute-start.7 = (bf16[256,256]{1,0:T(8,128)(2,1)S(1)}, bf16[256,256]{1,0:T(8,128)(2,1)S(1)}, u32[]{:S(2)}, u32[]{:S(2)}) collective-permute-start(bf16[256,256]{1,0:T(8,128)(2,1)S(1)} %pad_maximum_fusion.2), channel_id=1, source_target_pairs={{36,4},{44,12},{52,20},{60,28},{64,0},{68,36},{72,8},{76,44},{80,1... | collective-permute-start | bytes 393224 | tf_op jit(solution)/shard_map/ppermute | solution.py:182
  63.1 4.0 %collective-permute-start.8 = (bf16[256,256]{1,0:T(8,128)(2,1)S(1)}, bf16[256,256]{1,0:T(8,128)(2,1)S(1)}, u32[]{:S(2)}, u32[]{:S(2)}) collective-permute-start(bf16[256,256]{1,0:T(8,128)(2,1)S(1)} %pad_maximum_fusion.3), channel_id=1, source_target_pairs={{12,4},{16,0},{20,12},{24,8},{28,20},{32,16},{36,28},{40,24},{44,3... | collective-permute-start | bytes 393224 | tf_op jit(solution)/shard_map/ppermute | solution.py:182
  67.1 18.2 %collective-permute-done.6.a1_ref = bf16[256,256]{1,0:T(8,128)(2,1)S(1)} collective-permute-done((bf16[256,256]{1,0:T(8,128)(2,1)S(1)}, bf16[256,256]{1,0:T(8,128)(2,1)S(1)}, u32[]{:S(2)}, u32[]{:S(2)}) %collective-permute-start.6) | collective-permute-done | bytes 131104 | tf_op jit(solution)/shard_map/ppermute | solution.py:182
  85.3 0.0 collective-permute-done.7.a2_ref
  85.3 0.0 collective-permute-done.8.a3_ref
  85.3 1.9 %collective-permute-start.9 = (bf16[128,256]{1,0:T(8,128)(2,1)S(1)}, bf16[128,256]{1,0:T(8,128)(2,1)S(1)}, u32[]{:S(2)}, u32[]{:S(2)}) collective-permute-start(bf16[128,256]{1,0:T(8,128)(2,1)S(1)} %add_convert_fusion), channel_id=1, source_target_pairs={{0,4},{4,0},{8,12},{12,8},{16,20},{20,16},{24,28},{28,24},{32,36},... | collective-permute-start | bytes 196616 | tf_op jit(solution)/shard_map/ppermute | solution.py:173
  87.3 1.2 %collective-permute-done.9.t_ref = bf16[128,256]{1,0:T(8,128)(2,1)S(1)} collective-permute-done((bf16[128,256]{1,0:T(8,128)(2,1)S(1)}, bf16[128,256]{1,0:T(8,128)(2,1)S(1)}, u32[]{:S(2)}, u32[]{:S(2)}) %collective-permute-start.9) | collective-permute-done | bytes 65568 | tf_op jit(solution)/shard_map/ppermute | solution.py:173
  88.5 0.0 copy-done
  88.5 0.0 copy-done.1
  88.5 0.7 shard_map.90
  89.2 18.0 %all_to_all.11 = bf16[4,128,896]{2,1,0:T(8,128)(2,1)S(1)} all-to-all(bf16[4,128,896]{2,1,0:T(8,128)(2,1)S(1)} %bitcast.5), channel_id=1, replica_groups=mesh['ctx'=128,'head'=4] {'head'}, dimensions={0} | all-to-all | bytes 1835008 | tf_op jit(solution)/shard_map/all_to_all | solution.py:249
  107.3 0.8 shard_map.91
  (11 shorter events, 0.2 us)
Async XLA Ops:
  17.5 3.1 %collective-permute-start = (bf16[128,256]{1,0:T(8,128)(2,1)S(1)}, bf16[128,256]{1,0:T(8,128)(2,1)S(1)}, u32[]{:S(2)}, u32[]{:S(2)}) collective-permute-start(bf16[128,256]{1,0:T(8,128)(2,1)S(1)} %shard_map.85.own_ref), channel_id=1, source_target_pairs={{0,4},{4,0},{8,12},{12,8},{16,20},{20,16},{24,28},{28,24},{32,36},... | collective-permute-start | bytes 196616 | tf_op jit(solution)/shard_map/ppermute | solution.py:173
  20.6 21.8 %collective-permute-start.1 = (bf16[256,256]{1,0:T(8,128)(2,1)S(1)}, bf16[256,256]{1,0:T(8,128)(2,1)S(1)}, u32[]{:S(2)}, u32[]{:S(2)}) collective-permute-start(bf16[256,256]{1,0:T(8,128)(2,1)S(1)} %pad_maximum_fusion), channel_id=1, source_target_pairs={{0,256},{4,132},{8,264},{12,140},{16,272},{20,148},{24,280},{28,15... | collective-permute-start | bytes 393224 | tf_op jit(solution)/shard_map/ppermute | solution.py:182
  35.5 7.3 %collective-permute-start.2 = (bf16[256,256]{1,0:T(8,128)(2,1)S(1)}, bf16[256,256]{1,0:T(8,128)(2,1)S(1)}, u32[]{:S(2)}, u32[]{:S(2)}) collective-permute-start(bf16[256,256]{1,0:T(8,128)(2,1)S(1)} %pad_maximum_fusion), channel_id=1, source_target_pairs={{0,64},{4,36},{8,72},{12,44},{16,80},{20,52},{24,88},{28,60},{32,9... | collective-permute-start | bytes 393224 | tf_op jit(solution)/shard_map/ppermute | solution.py:182
  38.8 8.4 %collective-permute-start.3 = (bf16[256,256]{1,0:T(8,128)(2,1)S(1)}, bf16[256,256]{1,0:T(8,128)(2,1)S(1)}, u32[]{:S(2)}, u32[]{:S(2)}) collective-permute-start(bf16[256,256]{1,0:T(8,128)(2,1)S(1)} %pad_maximum_fusion), channel_id=1, source_target_pairs={{0,16},{4,12},{8,24},{12,20},{16,32},{20,28},{24,40},{28,36},{32,4... | collective-permute-start | bytes 393224 | tf_op jit(solution)/shard_map/ppermute | solution.py:182
  42.7 7.9 %copy-start.2 = (bf16[128,896]{1,0:T(8,128)(2,1)S(1)}, bf16[128,896]{1,0:T(8,128)(2,1)}, u32[]{:S(2)}) copy-start(bf16[128,896]{1,0:T(8,128)(2,1)} %q_ref.1) | copy-start | bytes 688132
  42.7 7.9 %copy-start.3 = (bf16[128,896]{1,0:T(8,128)(2,1)S(1)}, bf16[128,896]{1,0:T(8,128)(2,1)}, u32[]{:S(2)}) copy-start(bf16[128,896]{1,0:T(8,128)(2,1)} %c_ref.1) | copy-start | bytes 688132
  47.2 3.4 %collective-permute-start.4 = (bf16[512,256]{1,0:T(8,128)(2,1)S(1)}, bf16[512,256]{1,0:T(8,128)(2,1)S(1)}, u32[]{:S(2)}, u32[]{:S(2)}) collective-permute-start(bf16[512,256]{1,0:T(8,128)(2,1)S(1)} %shard_map.88), channel_id=1, source_target_pairs={{0,4},{4,0},{8,12},{12,8},{16,20},{20,16},{24,28},{28,24},{32,36},... | collective-permute-start | bytes 786440 | tf_op jit(solution)/shard_map/ppermute | solution.py:173
  56.9 3.4 %collective-permute-start.5 = (bf16[512,256]{1,0:T(8,128)(2,1)S(1)}, bf16[512,256]{1,0:T(8,128)(2,1)S(1)}, u32[]{:S(2)}, u32[]{:S(2)}) collective-permute-start(bf16[512,256]{1,0:T(8,128)(2,1)S(1)} %get-tuple-element.11), channel_id=1, source_target_pairs={{0,4},{4,0},{8,12},{12,8},{16,20},{20,16},{24,28},{28,24},{32,36},... | collective-permute-start | bytes 786440 | tf_op jit(solution)/shard_map/ppermute | solution.py:173
  59.0 29.5 %copy-start = (bf16[3584,128]{1,0:T(8,128)(2,1)S(1)}, bf16[3584,128]{1,0:T(8,128)(2,1)}, u32[]{:S(2)}) copy-start(bf16[3584,128]{1,0:T(8,128)(2,1)} %wk_ref.1) | copy-start | bytes 2752516
  59.0 29.5 %copy-start.1 = (bf16[3584,128]{1,0:T(8,128)(2,1)S(1)}, bf16[3584,128]{1,0:T(8,128)(2,1)}, u32[]{:S(2)}) copy-start(bf16[3584,128]{1,0:T(8,128)(2,1)} %wv_ref.1) | copy-start | bytes 2752516
  60.4 24.9 %collective-permute-start.6 = (bf16[256,256]{1,0:T(8,128)(2,1)S(1)}, bf16[256,256]{1,0:T(8,128)(2,1)S(1)}, u32[]{:S(2)}, u32[]{:S(2)}) collective-permute-start(bf16[256,256]{1,0:T(8,128)(2,1)S(1)} %pad_maximum_fusion.1), channel_id=1, source_target_pairs={{132,4},{140,12},{148,20},{156,28},{164,36},{172,44},{180,52},{188... | collective-permute-start | bytes 393224 | tf_op jit(solution)/shard_map/ppermute | solution.py:182
  61.7 23.6 %collective-permute-start.7 = (bf16[256,256]{1,0:T(8,128)(2,1)S(1)}, bf16[256,256]{1,0:T(8,128)(2,1)S(1)}, u32[]{:S(2)}, u32[]{:S(2)}) collective-permute-start(bf16[256,256]{1,0:T(8,128)(2,1)S(1)} %pad_maximum_fusion.2), channel_id=1, source_target_pairs={{36,4},{44,12},{52,20},{60,28},{64,0},{68,36},{72,8},{76,44},{80,1... | collective-permute-start | bytes 393224 | tf_op jit(solution)/shard_map/ppermute | solution.py:182
  63.1 22.2 %collective-permute-start.8 = (bf16[256,256]{1,0:T(8,128)(2,1)S(1)}, bf16[256,256]{1,0:T(8,128)(2,1)S(1)}, u32[]{:S(2)}, u32[]{:S(2)}) collective-permute-start(bf16[256,256]{1,0:T(8,128)(2,1)S(1)} %pad_maximum_fusion.3), channel_id=1, source_target_pairs={{12,4},{16,0},{20,12},{24,8},{28,20},{32,16},{36,28},{40,24},{44,3... | collective-permute-start | bytes 393224 | tf_op jit(solution)/shard_map/ppermute | solution.py:182
  85.3 3.1 %collective-permute-start.9 = (bf16[128,256]{1,0:T(8,128)(2,1)S(1)}, bf16[128,256]{1,0:T(8,128)(2,1)S(1)}, u32[]{:S(2)}, u32[]{:S(2)}) collective-permute-start(bf16[128,256]{1,0:T(8,128)(2,1)S(1)} %add_convert_fusion), channel_id=1, source_target_pairs={{0,4},{4,0},{8,12},{12,8},{16,20},{20,16},{24,28},{28,24},{32,36},... | collective-permute-start | bytes 196616 | tf_op jit(solution)/shard_map/ppermute | solution.py:173

commit v3 on v2

--- a/solution.py
+++ b/solution.py
@@ -118,7 +118,7 @@
             target[row * B : (row + 1) * B, HEAD_DIM:] = dvalue.astype(jnp.bfloat16)
 
 
-def finish_kernel(place_ref, local_ref, swap_ref, a1_ref, a2_ref, a3_ref, t_ref, wk_ref, wv_ref, out_ref):
+def total_kernel(place_ref, local_ref, swap_ref, a1_ref, a2_ref, a3_ref, t_ref, out_ref):
     core = lax.rem(place_ref[0], 2)
     B = BLOCK
     total = local_ref[...]
@@ -126,19 +126,17 @@
     for ref in (a1_ref, a2_ref, a3_ref):
         total += ref[:B, :].astype(jnp.float32)
     total = (total + t_ref[...].astype(jnp.float32)).astype(jnp.bfloat16)
-    width = wk_ref.shape[0] // 4
     for part in range(4):
-        rows = slice(part * width, (part + 1) * width)
-        term = dot(total[:, :HEAD_DIM], wk_ref[rows, :], DIMS_NT)
-        term += dot(total[:, HEAD_DIM:], wv_ref[rows, :], DIMS_NT)
-        out_ref[part * B : (part + 1) * B, :] = term.astype(jnp.bfloat16)
-
-
-def add_kernel(parts_ref, out_ref):
-    B = BLOCK
-    total = parts_ref[:B, :].astype(jnp.float32)
-    for part in range(1, 4):
-        total += parts_ref[part * B : (part + 1) * B, :].astype(jnp.float32)
+        out_ref[part * B : (part + 1) * B, :] = total
+
+
+def finish_kernel(grads_ref, slabs_ref, out_ref):
+    B = BLOCK
+    total = jnp.zeros(out_ref.shape, jnp.float32)
+    for part in range(4):
+        for side in range(2):
+            grads = grads_ref[part * B : (part + 1) * B, side * HEAD_DIM : (side + 1) * HEAD_DIM]
+            total += dot(grads, slabs_ref[part, side], DIMS_NT)
     out_ref[...] = total.astype(jnp.bfloat16)
 
 
@@ -204,6 +202,10 @@
     )
     sibling = swap(own, count)
     pair = jnp.concatenate([own, sibling], axis=0)
+    depth = w_key.shape[0] // 4
+    slab_shape = (4, depth, HEAD_DIM)
+    key_rows, value_rows, pair = lax.optimization_barrier((w_key, w_value, pair))
+    slabs = jnp.stack([key_rows.reshape(slab_shape), value_rows.reshape(slab_shape)], axis=1)
     r1 = shift(pair, count, 64, 32)
     r2 = shift(pair, count, 16, 8)
     r3 = shift(pair, count, 4, 2)
@@ -229,6 +231,8 @@
         ),
         flops=12 * width * 8 * B * HEAD_DIM,
     )
+    far, slabs = lax.optimization_barrier((far, slabs))
+    slabs = lax.all_to_all(slabs, "head", 0, 0, tiled=True)
     back = swap(far, count)
     m1 = jnp.concatenate([near[:B], back[:B]], axis=0)
     m2 = jnp.concatenate([near[B : 2 * B], back[B : 2 * B]], axis=0)
@@ -240,14 +244,19 @@
     a3 = shift(m3, count, -4, -2)
     across = a1[B:].astype(jnp.float32) + a2[B:].astype(jnp.float32) + a3[B:].astype(jnp.float32)
     last = swap(across.astype(bf16), count)
-    terms = call(
+    last, slabs = lax.optimization_barrier((last, slabs))
+    total = call(
+        total_kernel,
+        jax.ShapeDtypeStruct((4 * B, 2 * HEAD_DIM), bf16),
+        (place, local, back, a1, a2, a3, last),
+    )
+    arrived = lax.all_to_all(total, "head", 0, 0, tiled=True)
+    input_grad = call(
         finish_kernel,
-        jax.ShapeDtypeStruct((4 * B, width), bf16),
-        (place, local, back, a1, a2, a3, last, w_key, w_value),
-        flops=4 * B * 4 * width * HEAD_DIM,
-    )
-    arrived = lax.all_to_all(terms, "head", 0, 0, tiled=True)
-    input_grad = call(add_kernel, jax.ShapeDtypeStruct((B, width), bf16), (arrived,))
+        jax.ShapeDtypeStruct((B, width), bf16),
+        (arrived, slabs),
+        flops=16 * B * width * HEAD_DIM,
+    )
     return (attended, query_grad, input_grad)
 
 

time: 108 us -> 106 us (0.981)
  the two profiles are of different devices: /device:TPU:56 before, /device:TPU:48 now
where the time goes in v3:
time: 106 us; the launch traced here: 105 us
  starting transfers between devices  39 us (37%)
  waiting for transfers between devices  27.9 us (26%)
  blocking collectives  26 us (25%)
  Pallas kernels  9.96 us (9%)
  other arithmetic  1.51 us (1%)
    ppermute x6, starting transfers between devices, shift(): return lax.ppermute(value, 'ctx', pairs)  26.6 us
    ppermute x6, waiting for transfers between devices, shift(): return lax.ppermute(value, 'ctx', pairs)  25.4 us
    all_gather x1, blocking collectives, shards(): rows = lax.all_gather(inputs, 'head', axis=1, tiled=True)  14.8 us
    all_to_all x1, blocking collectives, shards(): arrived = lax.all_to_all(total, 'head', 0, 0, tiled=True)  11.2 us
    pallas_call x7, Pallas kernels, call(): pl.pallas_call(kernel, out_shape=out_shape, in_specs=specs, out_specs=jax...  9.96 us
    ppermute x4, starting transfers between devices, swap(): return lax.ppermute(value, 'ctx', [(i, i ^ 1) for i in range(count)])  8.15 us
    all_to_all x1, starting transfers between devices, shards(): slabs = lax.all_to_all(slabs, 'head', 0, 0, tiled=True)  4.23 us
    ppermute x4, waiting for transfers between devices, swap(): return lax.ppermute(value, 'ctx', [(i, i ^ 1) for i in range(count)])  2.48 us
  transfers between devices with their start and end apart: 11, of which 6 were waited for; matrix products, arithmetic and copies ran while one was open for 1% of the time, Pallas kernels for 0%

profile of v3, /device:TPU:48, one launch (start us, length us, event | category | flops | bytes accessed | tf_op | source)
XLA Modules:
  0.0 105.3 jit_solution(15911815224580322192)
XLA Ops:
  0.6 14.8 %all_gather.3.x_ref = bf16[128,3584]{1,0:T(8,128)(2,1)S(1)} all-gather(bf16[128,896]{1,0:T(8,128)(2,1)} %param.6), channel_id=1, replica_groups=mesh['ctx'=128,'head'=4] {'head'}, dimensions={1}, use_global_device_ids=true | all-gather | bytes 1146880 | tf_op jit(solution)/shard_map/all_gather | solution.py:189
  15.5 0.0 copy-start.2
  15.5 0.0 copy-start.3
  15.5 2.2 %shard_map.85.own_ref = bf16[128,256]{1,0:T(8,128)(2,1)S(1)} custom-call(bf16[128,3584]{1,0:T(8,128)(2,1)S(1)} %all_gather.3.x_ref, bf16[3584,128]{1,0:T(8,128)(2,1)} %wk_hbm.1, bf16[3584,128]{1,0:T(8,128)(2,1)} %wv_hbm.1, bf16[1,128]{1,0:T(2,128)(2,1)} %bitcast.10), custom_call_target="tpu_custom_call" | custom-call | flops 234881024 | bytes 2752768 | tf_op jit(solution)/shard_map/pallas_call | solution.py:155
  17.7 1.9 %collective-permute-start = (bf16[128,256]{1,0:T(8,128)(2,1)S(1)}, bf16[128,256]{1,0:T(8,128)(2,1)S(1)}, u32[]{:S(2)}, u32[]{:S(2)}) collective-permute-start(bf16[128,256]{1,0:T(8,128)(2,1)S(1)} %shard_map.85.own_ref), channel_id=1, source_target_pairs={{0,4},{4,0},{8,12},{12,8},{16,20},{20,16},{24,28},{28,24},{32,36},... | collective-permute-start | bytes 196616 | tf_op jit(solution)/shard_map/ppermute | solution.py:171
  19.6 1.2 %collective-permute-done.sib_ref = bf16[128,256]{1,0:T(8,128)(2,1)S(1)} collective-permute-done((bf16[128,256]{1,0:T(8,128)(2,1)S(1)}, bf16[128,256]{1,0:T(8,128)(2,1)S(1)}, u32[]{:S(2)}, u32[]{:S(2)}) %collective-permute-start) | collective-permute-done | bytes 65568 | tf_op jit(solution)/shard_map/ppermute | solution.py:171
  20.8 14.8 %collective-permute-start.1 = (bf16[256,256]{1,0:T(8,128)(2,1)S(1)}, bf16[256,256]{1,0:T(8,128)(2,1)S(1)}, u32[]{:S(2)}, u32[]{:S(2)}) collective-permute-start(bf16[256,256]{1,0:T(8,128)(2,1)S(1)} %pad_maximum_fusion.1), channel_id=1, source_target_pairs={{0,256},{4,132},{8,264},{12,140},{16,272},{20,148},{24,280},{28,15... | collective-permute-start | bytes 393224 | tf_op jit(solution)/shard_map/ppermute | solution.py:180
  35.7 3.4 %collective-permute-start.2 = (bf16[256,256]{1,0:T(8,128)(2,1)S(1)}, bf16[256,256]{1,0:T(8,128)(2,1)S(1)}, u32[]{:S(2)}, u32[]{:S(2)}) collective-permute-start(bf16[256,256]{1,0:T(8,128)(2,1)S(1)} %pad_maximum_fusion.1), channel_id=1, source_target_pairs={{0,64},{4,36},{8,72},{12,44},{16,80},{20,52},{24,88},{28,60},{32,9... | collective-permute-start | bytes 393224 | tf_op jit(solution)/shard_map/ppermute | solution.py:180
  39.1 2.7 %collective-permute-start.3 = (bf16[256,256]{1,0:T(8,128)(2,1)S(1)}, bf16[256,256]{1,0:T(8,128)(2,1)S(1)}, u32[]{:S(2)}, u32[]{:S(2)}) collective-permute-start(bf16[256,256]{1,0:T(8,128)(2,1)S(1)} %pad_maximum_fusion.1), channel_id=1, source_target_pairs={{0,16},{4,12},{8,24},{12,20},{16,32},{20,28},{24,40},{28,36},{32,4... | collective-permute-start | bytes 393224 | tf_op jit(solution)/shard_map/ppermute | solution.py:180
  41.8 0.6 collective-permute-done.1.r1_ref
  42.4 0.5 collective-permute-done.2.r2_ref
  42.9 4.5 %collective-permute-done.3.r3_ref = bf16[256,256]{1,0:T(8,128)(2,1)S(1)} collective-permute-done((bf16[256,256]{1,0:T(8,128)(2,1)S(1)}, bf16[256,256]{1,0:T(8,128)(2,1)S(1)}, u32[]{:S(2)}, u32[]{:S(2)}) %collective-permute-start.3) | collective-permute-done | bytes 131104 | tf_op jit(solution)/shard_map/ppermute | solution.py:180
  47.5 1.9 %collective-permute-start.4 = (bf16[512,256]{1,0:T(8,128)(2,1)S(1)}, bf16[512,256]{1,0:T(8,128)(2,1)S(1)}, u32[]{:S(2)}, u32[]{:S(2)}) collective-permute-start(bf16[512,256]{1,0:T(8,128)(2,1)S(1)} %shard_map.88), channel_id=1, source_target_pairs={{0,4},{4,0},{8,12},{12,8},{16,20},{20,16},{24,28},{28,24},{32,36},... | collective-permute-start | bytes 786440 | tf_op jit(solution)/shard_map/ppermute | solution.py:171
  49.4 0.0 copy-done.2
  49.4 0.0 copy-done.3
  49.4 0.0 copy-start
  49.4 0.0 copy-start.1
  49.4 1.4 %pad_maximum_fusion = bf16[4,2,896,128]{3,2,1,0:T(8,128)(2,1)} fusion(bf16[4,1,896,128]{3,2,1,0:T(8,128)(2,1)S(1)} %bitcast.9, bf16[4,1,896,128]{3,2,1,0:T(8,128)(2,1)S(1)} %bitcast.8), kind=kLoop, calls=%fused_computation | loop fusion | flops 917504 | bytes 3670016 | tf_op jit(solution)/shard_map/stack | solution.py:208
  50.8 0.0 collective-permute-done.4.sw_ref
  50.9 0.0 copy-done
  50.9 0.0 copy-done.1
  50.9 6.3 %shard_map.89 = (bf16[128,896]{1,0:T(8,128)(2,1)}, bf16[128,896]{1,0:T(8,128)(2,1)}, f32[128,256]{1,0:T(8,128)S(1)}, bf16[384,256]{1,0:T(8,128)(2,1)S(1)}, bf16[512,256]{1,0:T(8,128)(2,1)S(1)}) custom-call(s32[1]{0:T(128)} %bitcast.place_ref, bf16[128,896]{1,0:T(8,128)(2,1)S(1)} %copy-done, bf16[128,896]{1,0:T(8,128)(2,1)S(1)} %copy-done.1, ...), custom_call_target="tpu_custom_call" | custom-call | flops 1409286144 | bytes 1245188 | tf_op jit(solution)/shard_map/pallas_call | solution.py:155
  57.2 2.4 %collective-permute-start.5 = (bf16[512,256]{1,0:T(8,128)(2,1)S(1)}, bf16[512,256]{1,0:T(8,128)(2,1)S(1)}, u32[]{:S(2)}, u32[]{:S(2)}) collective-permute-start(bf16[512,256]{1,0:T(8,128)(2,1)S(1)} %get-tuple-element.22), channel_id=1, source_target_pairs={{0,4},{4,0},{8,12},{12,8},{16,20},{20,16},{24,28},{28,24},{32,36},... | collective-permute-start | bytes 786440 | tf_op jit(solution)/shard_map/ppermute | solution.py:171
  59.6 4.2 %all-to-all-start = ((bf16[4,2,896,128]{3,2,1,0:T(8,128)(2,1)}), bf16[4,2,896,128]{3,2,1,0:T(8,128)(2,1)S(1)}, u32[]{:S(2)}, u32[]{:S(2)}) async-start(bf16[4,2,896,128]{3,2,1,0:T(8,128)(2,1)} %pad_maximum_fusion), calls=%async_computation | async-start | bytes 3670016 | tf_op jit(solution)/shard_map/all_to_all | solution.py:235
  63.8 0.0 collective-permute-done.5.swap_ref
  63.8 1.3 %collective-permute-start.6 = (bf16[256,256]{1,0:T(8,128)(2,1)S(1)}, bf16[256,256]{1,0:T(8,128)(2,1)S(1)}, u32[]{:S(2)}, u32[]{:S(2)}) collective-permute-start(bf16[256,256]{1,0:T(8,128)(2,1)S(1)} %pad_maximum_fusion.2), channel_id=1, source_target_pairs={{132,4},{140,12},{148,20},{156,28},{164,36},{172,44},{180,52},{188... | collective-permute-start | bytes 393224 | tf_op jit(solution)/shard_map/ppermute | solution.py:180
  65.2 1.3 %collective-permute-start.7 = (bf16[256,256]{1,0:T(8,128)(2,1)S(1)}, bf16[256,256]{1,0:T(8,128)(2,1)S(1)}, u32[]{:S(2)}, u32[]{:S(2)}) collective-permute-start(bf16[256,256]{1,0:T(8,128)(2,1)S(1)} %pad_maximum_fusion.3), channel_id=1, source_target_pairs={{36,4},{44,12},{52,20},{60,28},{64,0},{68,36},{72,8},{76,44},{80,1... | collective-permute-start | bytes 393224 | tf_op jit(solution)/shard_map/ppermute | solution.py:180
  66.5 3.1 %collective-permute-start.8 = (bf16[256,256]{1,0:T(8,128)(2,1)S(1)}, bf16[256,256]{1,0:T(8,128)(2,1)S(1)}, u32[]{:S(2)}, u32[]{:S(2)}) collective-permute-start(bf16[256,256]{1,0:T(8,128)(2,1)S(1)} %pad_maximum_fusion.4), channel_id=1, source_target_pairs={{12,4},{16,0},{20,12},{24,8},{28,20},{32,16},{36,28},{40,24},{44,3... | collective-permute-start | bytes 393224 | tf_op jit(solution)/shard_map/ppermute | solution.py:180
  69.7 19.7 %collective-permute-done.6.a1_ref = bf16[256,256]{1,0:T(8,128)(2,1)S(1)} collective-permute-done((bf16[256,256]{1,0:T(8,128)(2,1)S(1)}, bf16[256,256]{1,0:T(8,128)(2,1)S(1)}, u32[]{:S(2)}, u32[]{:S(2)}) %collective-permute-start.6) | collective-permute-done | bytes 131104 | tf_op jit(solution)/shard_map/ppermute | solution.py:180
  89.4 0.0 collective-permute-done.7.a2_ref
  89.4 0.0 collective-permute-done.8.a3_ref
  89.4 1.9 %collective-permute-start.9 = (bf16[128,256]{1,0:T(8,128)(2,1)S(1)}, bf16[128,256]{1,0:T(8,128)(2,1)S(1)}, u32[]{:S(2)}, u32[]{:S(2)}) collective-permute-start(bf16[128,256]{1,0:T(8,128)(2,1)S(1)} %add_convert_fusion), channel_id=1, source_target_pairs={{0,4},{4,0},{8,12},{12,8},{16,20},{20,16},{24,28},{28,24},{32,36},... | collective-permute-start | bytes 196616 | tf_op jit(solution)/shard_map/ppermute | solution.py:171
  91.4 1.2 %collective-permute-done.9.t_ref = bf16[128,256]{1,0:T(8,128)(2,1)S(1)} collective-permute-done((bf16[128,256]{1,0:T(8,128)(2,1)S(1)}, bf16[128,256]{1,0:T(8,128)(2,1)S(1)}, u32[]{:S(2)}, u32[]{:S(2)}) %collective-permute-start.9) | collective-permute-done | bytes 65568 | tf_op jit(solution)/shard_map/ppermute | solution.py:171
  92.6 0.0 all-to-all-done.slabs_ref
  92.6 0.1 shard_map.90
  92.6 11.2 %all_to_all.16 = bf16[4,128,256]{2,1,0:T(8,128)(2,1)S(1)} all-to-all(bf16[4,128,256]{2,1,0:T(8,128)(2,1)S(1)} %bitcast.7), channel_id=1, replica_groups=mesh['ctx'=128,'head'=4] {'head'}, dimensions={0} | all-to-all | bytes 524288 | tf_op jit(solution)/shard_map/all_to_all | solution.py:253
  103.9 1.4 %shard_map.91 = bf16[128,896]{1,0:T(8,128)(2,1)} custom-call(bf16[512,256]{1,0:T(8,128)(2,1)S(1)} %bitcast.6, bf16[4,2,896,128]{3,2,1,0:T(8,128)(2,1)S(1)} %all-to-all-done.slabs_ref), custom_call_target="tpu_custom_call" | custom-call | flops 234881024 | bytes 2097152 | tf_op jit(solution)/shard_map/pallas_call | solution.py:155
  (11 shorter events, 0.2 us)
Async XLA Ops:
  15.5 33.9 %copy-start.2 = (bf16[3584,128]{1,0:T(8,128)(2,1)S(1)}, bf16[3584,128]{1,0:T(8,128)(2,1)}, u32[]{:S(2)}) copy-start(bf16[3584,128]{1,0:T(8,128)(2,1)} %wk_hbm.1) | copy-start | bytes 2752516
  15.5 33.9 %copy-start.3 = (bf16[3584,128]{1,0:T(8,128)(2,1)S(1)}, bf16[3584,128]{1,0:T(8,128)(2,1)}, u32[]{:S(2)}) copy-start(bf16[3584,128]{1,0:T(8,128)(2,1)} %wv_hbm.1) | copy-start | bytes 2752516
  17.7 3.1 %collective-permute-start = (bf16[128,256]{1,0:T(8,128)(2,1)S(1)}, bf16[128,256]{1,0:T(8,128)(2,1)S(1)}, u32[]{:S(2)}, u32[]{:S(2)}) collective-permute-start(bf16[128,256]{1,0:T(8,128)(2,1)S(1)} %shard_map.85.own_ref), channel_id=1, source_target_pairs={{0,4},{4,0},{8,12},{12,8},{16,20},{20,16},{24,28},{28,24},{32,36},... | collective-permute-start | bytes 196616 | tf_op jit(solution)/shard_map/ppermute | solution.py:171
  20.8 21.5 %collective-permute-start.1 = (bf16[256,256]{1,0:T(8,128)(2,1)S(1)}, bf16[256,256]{1,0:T(8,128)(2,1)S(1)}, u32[]{:S(2)}, u32[]{:S(2)}) collective-permute-start(bf16[256,256]{1,0:T(8,128)(2,1)S(1)} %pad_maximum_fusion.1), channel_id=1, source_target_pairs={{0,256},{4,132},{8,264},{12,140},{16,272},{20,148},{24,280},{28,15... | collective-permute-start | bytes 393224 | tf_op jit(solution)/shard_map/ppermute | solution.py:180
  35.7 7.3 %collective-permute-start.2 = (bf16[256,256]{1,0:T(8,128)(2,1)S(1)}, bf16[256,256]{1,0:T(8,128)(2,1)S(1)}, u32[]{:S(2)}, u32[]{:S(2)}) collective-permute-start(bf16[256,256]{1,0:T(8,128)(2,1)S(1)} %pad_maximum_fusion.1), channel_id=1, source_target_pairs={{0,64},{4,36},{8,72},{12,44},{16,80},{20,52},{24,88},{28,60},{32,9... | collective-permute-start | bytes 393224 | tf_op jit(solution)/shard_map/ppermute | solution.py:180
  39.1 8.4 %collective-permute-start.3 = (bf16[256,256]{1,0:T(8,128)(2,1)S(1)}, bf16[256,256]{1,0:T(8,128)(2,1)S(1)}, u32[]{:S(2)}, u32[]{:S(2)}) collective-permute-start(bf16[256,256]{1,0:T(8,128)(2,1)S(1)} %pad_maximum_fusion.1), channel_id=1, source_target_pairs={{0,16},{4,12},{8,24},{12,20},{16,32},{20,28},{24,40},{28,36},{32,4... | collective-permute-start | bytes 393224 | tf_op jit(solution)/shard_map/ppermute | solution.py:180
  47.5 3.4 %collective-permute-start.4 = (bf16[512,256]{1,0:T(8,128)(2,1)S(1)}, bf16[512,256]{1,0:T(8,128)(2,1)S(1)}, u32[]{:S(2)}, u32[]{:S(2)}) collective-permute-start(bf16[512,256]{1,0:T(8,128)(2,1)S(1)} %shard_map.88), channel_id=1, source_target_pairs={{0,4},{4,0},{8,12},{12,8},{16,20},{20,16},{24,28},{28,24},{32,36},... | collective-permute-start | bytes 786440 | tf_op jit(solution)/shard_map/ppermute | solution.py:171
  49.4 1.5 %copy-start = (bf16[128,896]{1,0:T(8,128)(2,1)S(1)}, bf16[128,896]{1,0:T(8,128)(2,1)}, u32[]{:S(2)}) copy-start(bf16[128,896]{1,0:T(8,128)(2,1)} %q_ref.1) | copy-start | bytes 688132
  49.4 1.5 %copy-start.1 = (bf16[128,896]{1,0:T(8,128)(2,1)S(1)}, bf16[128,896]{1,0:T(8,128)(2,1)}, u32[]{:S(2)}) copy-start(bf16[128,896]{1,0:T(8,128)(2,1)} %c_ref.1) | copy-start | bytes 688132
  57.2 6.6 %collective-permute-start.5 = (bf16[512,256]{1,0:T(8,128)(2,1)S(1)}, bf16[512,256]{1,0:T(8,128)(2,1)S(1)}, u32[]{:S(2)}, u32[]{:S(2)}) collective-permute-start(bf16[512,256]{1,0:T(8,128)(2,1)S(1)} %get-tuple-element.22), channel_id=1, source_target_pairs={{0,4},{4,0},{8,12},{12,8},{16,20},{20,16},{24,28},{28,24},{32,36},... | collective-permute-start | bytes 786440 | tf_op jit(solution)/shard_map/ppermute | solution.py:171
  59.6 33.0 %all-to-all-start = ((bf16[4,2,896,128]{3,2,1,0:T(8,128)(2,1)}), bf16[4,2,896,128]{3,2,1,0:T(8,128)(2,1)S(1)}, u32[]{:S(2)}, u32[]{:S(2)}) async-start(bf16[4,2,896,128]{3,2,1,0:T(8,128)(2,1)} %pad_maximum_fusion), calls=%async_computation | async-start | bytes 3670016 | tf_op jit(solution)/shard_map/all_to_all | solution.py:235
  63.8 25.5 %collective-permute-start.6 = (bf16[256,256]{1,0:T(8,128)(2,1)S(1)}, bf16[256,256]{1,0:T(8,128)(2,1)S(1)}, u32[]{:S(2)}, u32[]{:S(2)}) collective-permute-start(bf16[256,256]{1,0:T(8,128)(2,1)S(1)} %pad_maximum_fusion.2), channel_id=1, source_target_pairs={{132,4},{140,12},{148,20},{156,28},{164,36},{172,44},{180,52},{188... | collective-permute-start | bytes 393224 | tf_op jit(solution)/shard_map/ppermute | solution.py:180
  65.2 24.2 %collective-permute-start.7 = (bf16[256,256]{1,0:T(8,128)(2,1)S(1)}, bf16[256,256]{1,0:T(8,128)(2,1)S(1)}, u32[]{:S(2)}, u32[]{:S(2)}) collective-permute-start(bf16[256,256]{1,0:T(8,128)(2,1)S(1)} %pad_maximum_fusion.3), channel_id=1, source_target_pairs={{36,4},{44,12},{52,20},{60,28},{64,0},{68,36},{72,8},{76,44},{80,1... | collective-permute-start | bytes 393224 | tf_op jit(solution)/shard_map/ppermute | solution.py:180
  66.5 22.9 %collective-permute-start.8 = (bf16[256,256]{1,0:T(8,128)(2,1)S(1)}, bf16[256,256]{1,0:T(8,128)(2,1)S(1)}, u32[]{:S(2)}, u32[]{:S(2)}) collective-permute-start(bf16[256,256]{1,0:T(8,128)(2,1)S(1)} %pad_maximum_fusion.4), channel_id=1, source_target_pairs={{12,4},{16,0},{20,12},{24,8},{28,20},{32,16},{36,28},{40,24},{44,3... | collective-permute-start | bytes 393224 | tf_op jit(solution)/shard_map/ppermute | solution.py:180
  89.4 3.1 %collective-permute-start.9 = (bf16[128,256]{1,0:T(8,128)(2,1)S(1)}, bf16[128,256]{1,0:T(8,128)(2,1)S(1)}, u32[]{:S(2)}, u32[]{:S(2)}) collective-permute-start(bf16[128,256]{1,0:T(8,128)(2,1)S(1)} %add_convert_fusion), channel_id=1, source_target_pairs={{0,4},{4,0},{8,12},{12,8},{16,20},{20,16},{24,28},{28,24},{32,36},... | collective-permute-start | bytes 196616 | tf_op jit(solution)/shard_map/ppermute | solution.py:171

commit v4 on v3

--- a/solution.py
+++ b/solution.py
@@ -6,10 +6,12 @@
 from jax import lax
 from jax.experimental import pallas as pl
 from jax.experimental.pallas import tpu as pltpu
+from jax.sharding import Mesh
 from jax.sharding import PartitionSpec as P
 
 HEAD_DIM = 128
 BLOCK = 128
+CTX = ("pair", "core")
 DIMS_NT = (((1,), (1,)), ((), ()))
 DIMS_TN = (((0,), (0,)), ((), ()))
 DIMS_NN = (((1,), (0,)), ((), ()))
@@ -118,25 +120,32 @@
             target[row * B : (row + 1) * B, HEAD_DIM:] = dvalue.astype(jnp.bfloat16)
 
 
-def total_kernel(place_ref, local_ref, swap_ref, a1_ref, a2_ref, a3_ref, t_ref, out_ref):
+def total_kernel(place_ref, local_ref, swap_ref, a1_ref, a2_ref, a3_ref, out_ref):
     core = lax.rem(place_ref[0], 2)
     B = BLOCK
     total = local_ref[...]
     total += jnp.where(core == 0, swap_ref[3 * B :, :].astype(jnp.float32), 0.0)
+    across = jnp.zeros(total.shape, jnp.float32)
     for ref in (a1_ref, a2_ref, a3_ref):
         total += ref[:B, :].astype(jnp.float32)
-    total = (total + t_ref[...].astype(jnp.float32)).astype(jnp.bfloat16)
-    for part in range(4):
-        out_ref[part * B : (part + 1) * B, :] = total
+        across += ref[B:, :].astype(jnp.float32)
+    for side in range(2):
+        value = jnp.where(core == side, total, across).astype(jnp.bfloat16)
+        for part in range(4):
+            row = (side * 4 + part) * B
+            out_ref[row : row + B, :] = value
 
 
 def finish_kernel(grads_ref, slabs_ref, out_ref):
     B = BLOCK
     total = jnp.zeros(out_ref.shape, jnp.float32)
     for part in range(4):
+        even = grads_ref[part * B : (part + 1) * B, :].astype(jnp.float32)
+        odd = grads_ref[(part + 4) * B : (part + 5) * B, :].astype(jnp.float32)
+        grads = (even + odd).astype(jnp.bfloat16)
         for side in range(2):
-            grads = grads_ref[part * B : (part + 1) * B, side * HEAD_DIM : (side + 1) * HEAD_DIM]
-            total += dot(grads, slabs_ref[part, side], DIMS_NT)
+            half = grads[:, side * HEAD_DIM : (side + 1) * HEAD_DIM]
+            total += dot(half, slabs_ref[part, side], DIMS_NT)
     out_ref[...] = total.astype(jnp.bfloat16)
 
 
@@ -168,7 +177,7 @@
 
 
 def swap(value, count):
-    return lax.ppermute(value, "ctx", [(i, i ^ 1) for i in range(count)])
+    return lax.ppermute(value, CTX, [(i, i ^ 1) for i in range(count)])
 
 
 def shift(value, count, even, odd):
@@ -177,12 +186,12 @@
         to = i + (even if i % 2 == 0 else odd)
         if 0 <= to < count:
             pairs.append((i, to))
-    return lax.ppermute(value, "ctx", pairs)
+    return lax.ppermute(value, CTX, pairs)
 
 
 def shards(inputs, queries, w_key, w_value, v_bias, cotangent):
-    count = lax.axis_size("ctx")
-    place = lax.axis_index("ctx").astype(jnp.int32).reshape(1)
+    count = lax.axis_size("pair") * 2
+    place = lax.axis_index(CTX).astype(jnp.int32).reshape(1)
     B = BLOCK
     bf16 = jnp.bfloat16
     width = queries.shape[1]
@@ -242,15 +251,13 @@
     a1 = shift(m1, count, -64, -32)
     a2 = shift(m2, count, -16, -8)
     a3 = shift(m3, count, -4, -2)
-    across = a1[B:].astype(jnp.float32) + a2[B:].astype(jnp.float32) + a3[B:].astype(jnp.float32)
-    last = swap(across.astype(bf16), count)
-    last, slabs = lax.optimization_barrier((last, slabs))
     total = call(
         total_kernel,
-        jax.ShapeDtypeStruct((4 * B, 2 * HEAD_DIM), bf16),
-        (place, local, back, a1, a2, a3, last),
-    )
-    arrived = lax.all_to_all(total, "head", 0, 0, tiled=True)
+        jax.ShapeDtypeStruct((8 * B, 2 * HEAD_DIM), bf16),
+        (place, local, back, a1, a2, a3),
+    )
+    total, slabs = lax.optimization_barrier((total, slabs))
+    arrived = lax.all_to_all(total, ("core", "head"), 0, 0, tiled=True)
     input_grad = call(
         finish_kernel,
         jax.ShapeDtypeStruct((B, width), bf16),
@@ -263,15 +270,15 @@
 def solution(mesh):
     return jax.shard_map(
         shards,
-        mesh=mesh,
+        mesh=Mesh(mesh.devices.reshape(-1, 2, mesh.devices.shape[1]), ("pair", "core", "head")),
         in_specs=(
-            P("ctx", "head"),
-            P("ctx", "head"),
+            P(CTX, "head"),
+            P(CTX, "head"),
             P(None, "head"),
             P(None, "head"),
             P("head"),
-            P("ctx", "head"),
-        ),
-        out_specs=(P("ctx", "head"), P("ctx", "head"), P("ctx", "head")),
+            P(CTX, "head"),
+        ),
+        out_specs=(P(CTX, "head"), P(CTX, "head"), P(CTX, "head")),
         check_vma=False,
     )

time: 106 us -> 106 us (level)
  the two profiles are of different devices: /device:TPU:48 before, /device:TPU:56 now
where the time goes in v4:
time: 106 us
  starting transfers between devices  38.6 us (36%)
  blocking collectives  29.2 us (28%)
  waiting for transfers between devices  25.5 us (24%)
  Pallas kernels  10 us (9%)
  other arithmetic  1.49 us (1%)
    ppermute x6, starting transfers between devices, shift(): return lax.ppermute(value, CTX, pairs)  28.4 us
    ppermute x6, waiting for transfers between devices, shift(): return lax.ppermute(value, CTX, pairs)  23 us
    all_gather x1, blocking collectives, shards(): rows = lax.all_gather(inputs, 'head', axis=1, tiled=True)  14.8 us
    all_to_all x1, blocking collectives, shards(): arrived = lax.all_to_all(total, ('core', 'head'), 0, 0, tiled=True)  14.3 us
    pallas_call x7, Pallas kernels, call(): pl.pallas_call(kernel, out_shape=out_shape, in_specs=specs, out_specs=jax...  10 us
    ppermute x3, starting transfers between devices, swap(): return lax.ppermute(value, CTX, [(i, i ^ 1) for i in range(count)])  5.94 us
    all_to_all x1, starting transfers between devices, shards(): slabs = lax.all_to_all(slabs, 'head', 0, 0, tiled=True)  4.23 us
    ppermute x3, waiting for transfers between devices, swap(): return lax.ppermute(value, CTX, [(i, i ^ 1) for i in range(count)])  2.52 us
  transfers between devices with their start and end apart: 10, of which 5 were waited for; matrix products, arithmetic and copies ran while one was open for 1% of the time, Pallas kernels for 0%

profile of v4, /device:TPU:56, one launch (start us, length us, event | category | flops | bytes accessed | tf_op | source)
XLA Modules:
  0.0 105.7 jit_solution(4071467291717448680)
XLA Ops:
  0.6 14.8 %all_gather.3.x_ref = bf16[128,3584]{1,0:T(8,128)(2,1)S(1)} all-gather(bf16[128,896]{1,0:T(8,128)(2,1)} %param.6), channel_id=1, replica_groups=mesh['pair'=64,'core'=2,'head'=4] {'head'}, dimensions={1}, use_global_device_ids=true | all-gather | bytes 1146880 | tf_op jit(solution)/shard_map/all_gather | solution.py:198
  15.5 0.0 copy-start.2
  15.5 0.0 copy-start.3
  15.5 2.2 %shard_map.85.own_ref = bf16[128,256]{1,0:T(8,128)(2,1)S(1)} custom-call(bf16[128,3584]{1,0:T(8,128)(2,1)S(1)} %all_gather.3.x_ref, bf16[3584,128]{1,0:T(8,128)(2,1)} %wk_hbm.1, bf16[3584,128]{1,0:T(8,128)(2,1)} %wv_hbm.1, bf16[1,128]{1,0:T(2,128)(2,1)} %bitcast.10), custom_call_target="tpu_custom_call" | custom-call | flops 234881024 | bytes 2752768 | tf_op jit(solution)/shard_map/pallas_call | solution.py:164
  17.7 1.9 %collective-permute-start = (bf16[128,256]{1,0:T(8,128)(2,1)S(1)}, bf16[128,256]{1,0:T(8,128)(2,1)S(1)}, u32[]{:S(2)}, u32[]{:S(2)}) collective-permute-start(bf16[128,256]{1,0:T(8,128)(2,1)S(1)} %shard_map.85.own_ref), channel_id=1, source_target_pairs={{0,4},{4,0},{8,12},{12,8},{16,20},{20,16},{24,28},{28,24},{32,36},... | collective-permute-start | bytes 196616 | tf_op jit(solution)/shard_map/ppermute | solution.py:180
  19.6 1.2 %collective-permute-done.sib_ref = bf16[128,256]{1,0:T(8,128)(2,1)S(1)} collective-permute-done((bf16[128,256]{1,0:T(8,128)(2,1)S(1)}, bf16[128,256]{1,0:T(8,128)(2,1)S(1)}, u32[]{:S(2)}, u32[]{:S(2)}) %collective-permute-start) | collective-permute-done | bytes 65568 | tf_op jit(solution)/shard_map/ppermute | solution.py:180
  20.8 14.8 %collective-permute-start.1 = (bf16[256,256]{1,0:T(8,128)(2,1)S(1)}, bf16[256,256]{1,0:T(8,128)(2,1)S(1)}, u32[]{:S(2)}, u32[]{:S(2)}) collective-permute-start(bf16[256,256]{1,0:T(8,128)(2,1)S(1)} %pad_maximum_fusion.1), channel_id=1, source_target_pairs={{0,256},{4,132},{8,264},{12,140},{16,272},{20,148},{24,280},{28,15... | collective-permute-start | bytes 393224 | tf_op jit(solution)/shard_map/ppermute | solution.py:189
  35.7 3.4 %collective-permute-start.2 = (bf16[256,256]{1,0:T(8,128)(2,1)S(1)}, bf16[256,256]{1,0:T(8,128)(2,1)S(1)}, u32[]{:S(2)}, u32[]{:S(2)}) collective-permute-start(bf16[256,256]{1,0:T(8,128)(2,1)S(1)} %pad_maximum_fusion.1), channel_id=1, source_target_pairs={{0,64},{4,36},{8,72},{12,44},{16,80},{20,52},{24,88},{28,60},{32,9... | collective-permute-start | bytes 393224 | tf_op jit(solution)/shard_map/ppermute | solution.py:189
  39.1 3.6 %collective-permute-start.3 = (bf16[256,256]{1,0:T(8,128)(2,1)S(1)}, bf16[256,256]{1,0:T(8,128)(2,1)S(1)}, u32[]{:S(2)}, u32[]{:S(2)}) collective-permute-start(bf16[256,256]{1,0:T(8,128)(2,1)S(1)} %pad_maximum_fusion.1), channel_id=1, source_target_pairs={{0,16},{4,12},{8,24},{12,20},{16,32},{20,28},{24,40},{28,36},{32,4... | collective-permute-start | bytes 393224 | tf_op jit(solution)/shard_map/ppermute | solution.py:189
  42.7 0.0 collective-permute-done.1.r1_ref
  42.7 0.2 collective-permute-done.2.r2_ref
  42.9 4.5 %collective-permute-done.3.r3_ref = bf16[256,256]{1,0:T(8,128)(2,1)S(1)} collective-permute-done((bf16[256,256]{1,0:T(8,128)(2,1)S(1)}, bf16[256,256]{1,0:T(8,128)(2,1)S(1)}, u32[]{:S(2)}, u32[]{:S(2)}) %collective-permute-start.3) | collective-permute-done | bytes 131104 | tf_op jit(solution)/shard_map/ppermute | solution.py:189
  47.5 1.9 %collective-permute-start.4 = (bf16[512,256]{1,0:T(8,128)(2,1)S(1)}, bf16[512,256]{1,0:T(8,128)(2,1)S(1)}, u32[]{:S(2)}, u32[]{:S(2)}) collective-permute-start(bf16[512,256]{1,0:T(8,128)(2,1)S(1)} %shard_map.88), channel_id=1, source_target_pairs={{0,4},{4,0},{8,12},{12,8},{16,20},{20,16},{24,28},{28,24},{32,36},... | collective-permute-start | bytes 786440 | tf_op jit(solution)/shard_map/ppermute | solution.py:180
  49.4 0.0 copy-done.2
  49.4 0.0 copy-done.3
  49.4 0.0 copy-start
  49.4 0.0 copy-start.1
  49.4 1.4 %pad_maximum_fusion = bf16[4,2,896,128]{3,2,1,0:T(8,128)(2,1)} fusion(bf16[4,1,896,128]{3,2,1,0:T(8,128)(2,1)S(1)} %bitcast.9, bf16[4,1,896,128]{3,2,1,0:T(8,128)(2,1)S(1)} %bitcast.8), kind=kLoop, calls=%fused_computation | loop fusion | flops 917504 | bytes 3670016 | tf_op jit(solution)/shard_map/stack | solution.py:217
  50.9 0.0 collective-permute-done.4.sw_ref
  50.9 0.0 copy-done
  50.9 0.0 copy-done.1
  50.9 6.3 %shard_map.89 = (bf16[128,896]{1,0:T(8,128)(2,1)}, bf16[128,896]{1,0:T(8,128)(2,1)}, f32[128,256]{1,0:T(8,128)S(1)}, bf16[384,256]{1,0:T(8,128)(2,1)S(1)}, bf16[512,256]{1,0:T(8,128)(2,1)S(1)}) custom-call(s32[1]{0:T(128)} %bitcast.place_ref, bf16[128,896]{1,0:T(8,128)(2,1)S(1)} %copy-done, bf16[128,896]{1,0:T(8,128)(2,1)S(1)} %copy-done.1, ...), custom_call_target="tpu_custom_call" | custom-call | flops 1409286144 | bytes 1245188 | tf_op jit(solution)/shard_map/pallas_call | solution.py:164
  57.2 4.2 %all-to-all-start = ((bf16[4,2,896,128]{3,2,1,0:T(8,128)(2,1)}), bf16[4,2,896,128]{3,2,1,0:T(8,128)(2,1)S(1)}, u32[]{:S(2)}, u32[]{:S(2)}) async-start(bf16[4,2,896,128]{3,2,1,0:T(8,128)(2,1)} %pad_maximum_fusion), calls=%async_computation | async-start | bytes 3670016 | tf_op jit(solution)/shard_map/all_to_all | solution.py:244
  61.4 2.1 %collective-permute-start.5 = (bf16[512,256]{1,0:T(8,128)(2,1)S(1)}, bf16[512,256]{1,0:T(8,128)(2,1)S(1)}, u32[]{:S(2)}, u32[]{:S(2)}) collective-permute-start(bf16[512,256]{1,0:T(8,128)(2,1)S(1)} %get-tuple-element.22), channel_id=1, source_target_pairs={{0,4},{4,0},{8,12},{12,8},{16,20},{20,16},{24,28},{28,24},{32,36},... | collective-permute-start | bytes 786440 | tf_op jit(solution)/shard_map/ppermute | solution.py:180
  63.5 1.3 %collective-permute-done.5.swap_ref = bf16[512,256]{1,0:T(8,128)(2,1)S(1)} collective-permute-done((bf16[512,256]{1,0:T(8,128)(2,1)S(1)}, bf16[512,256]{1,0:T(8,128)(2,1)S(1)}, u32[]{:S(2)}, u32[]{:S(2)}) %collective-permute-start.5) | collective-permute-done | bytes 262176 | tf_op jit(solution)/shard_map/ppermute | solution.py:180
  64.8 1.3 %collective-permute-start.6 = (bf16[256,256]{1,0:T(8,128)(2,1)S(1)}, bf16[256,256]{1,0:T(8,128)(2,1)S(1)}, u32[]{:S(2)}, u32[]{:S(2)}) collective-permute-start(bf16[256,256]{1,0:T(8,128)(2,1)S(1)} %pad_maximum_fusion.2), channel_id=1, source_target_pairs={{132,4},{140,12},{148,20},{156,28},{164,36},{172,44},{180,52},{188... | collective-permute-start | bytes 393224 | tf_op jit(solution)/shard_map/ppermute | solution.py:189
  66.2 1.3 %collective-permute-start.7 = (bf16[256,256]{1,0:T(8,128)(2,1)S(1)}, bf16[256,256]{1,0:T(8,128)(2,1)S(1)}, u32[]{:S(2)}, u32[]{:S(2)}) collective-permute-start(bf16[256,256]{1,0:T(8,128)(2,1)S(1)} %pad_maximum_fusion.3), channel_id=1, source_target_pairs={{36,4},{44,12},{52,20},{60,28},{64,0},{68,36},{72,8},{76,44},{80,1... | collective-permute-start | bytes 393224 | tf_op jit(solution)/shard_map/ppermute | solution.py:189
  67.5 4.0 %collective-permute-start.8 = (bf16[256,256]{1,0:T(8,128)(2,1)S(1)}, bf16[256,256]{1,0:T(8,128)(2,1)S(1)}, u32[]{:S(2)}, u32[]{:S(2)}) collective-permute-start(bf16[256,256]{1,0:T(8,128)(2,1)S(1)} %pad_maximum_fusion.4), channel_id=1, source_target_pairs={{12,4},{16,0},{20,12},{24,8},{28,20},{32,16},{36,28},{40,24},{44,3... | collective-permute-start | bytes 393224 | tf_op jit(solution)/shard_map/ppermute | solution.py:189
  71.6 18.3 %collective-permute-done.6.a1_ref = bf16[256,256]{1,0:T(8,128)(2,1)S(1)} collective-permute-done((bf16[256,256]{1,0:T(8,128)(2,1)S(1)}, bf16[256,256]{1,0:T(8,128)(2,1)S(1)}, u32[]{:S(2)}, u32[]{:S(2)}) %collective-permute-start.6) | collective-permute-done | bytes 131104 | tf_op jit(solution)/shard_map/ppermute | solution.py:189
  89.8 0.0 collective-permute-done.7.a2_ref
  89.8 0.0 collective-permute-done.8.a3_ref
  89.8 0.1 shard_map.90
  89.9 0.0 all-to-all-done.slabs_ref
  89.9 14.3 %all_to_all.16 = bf16[8,128,256]{2,1,0:T(8,128)(2,1)S(1)} all-to-all(bf16[8,128,256]{2,1,0:T(8,128)(2,1)S(1)} %bitcast.6), channel_id=1, replica_groups=mesh['pair'=64,'core'=2,'head'=4] {'core','head'}, dimensions={0} | all-to-all | bytes 1048576 | tf_op jit(solution)/shard_map/all_to_all | solution.py:260
  104.3 1.4 %shard_map.91 = bf16[128,896]{1,0:T(8,128)(2,1)} custom-call(bf16[1024,256]{1,0:T(8,128)(2,1)S(1)} %bitcast.7, bf16[4,2,896,128]{3,2,1,0:T(8,128)(2,1)S(1)} %all-to-all-done.slabs_ref), custom_call_target="tpu_custom_call" | custom-call | flops 234881024 | bytes 2359296 | tf_op jit(solution)/shard_map/pallas_call | solution.py:164
  (10 shorter events, 0.1 us)
Async XLA Ops:
  15.5 33.9 %copy-start.2 = (bf16[3584,128]{1,0:T(8,128)(2,1)S(1)}, bf16[3584,128]{1,0:T(8,128)(2,1)}, u32[]{:S(2)}) copy-start(bf16[3584,128]{1,0:T(8,128)(2,1)} %wk_hbm.1) | copy-start | bytes 2752516
  15.5 33.9 %copy-start.3 = (bf16[3584,128]{1,0:T(8,128)(2,1)S(1)}, bf16[3584,128]{1,0:T(8,128)(2,1)}, u32[]{:S(2)}) copy-start(bf16[3584,128]{1,0:T(8,128)(2,1)} %wv_hbm.1) | copy-start | bytes 2752516
  17.7 3.1 %collective-permute-start = (bf16[128,256]{1,0:T(8,128)(2,1)S(1)}, bf16[128,256]{1,0:T(8,128)(2,1)S(1)}, u32[]{:S(2)}, u32[]{:S(2)}) collective-permute-start(bf16[128,256]{1,0:T(8,128)(2,1)S(1)} %shard_map.85.own_ref), channel_id=1, source_target_pairs={{0,4},{4,0},{8,12},{12,8},{16,20},{20,16},{24,28},{28,24},{32,36},... | collective-permute-start | bytes 196616 | tf_op jit(solution)/shard_map/ppermute | solution.py:180
  20.8 21.8 %collective-permute-start.1 = (bf16[256,256]{1,0:T(8,128)(2,1)S(1)}, bf16[256,256]{1,0:T(8,128)(2,1)S(1)}, u32[]{:S(2)}, u32[]{:S(2)}) collective-permute-start(bf16[256,256]{1,0:T(8,128)(2,1)S(1)} %pad_maximum_fusion.1), channel_id=1, source_target_pairs={{0,256},{4,132},{8,264},{12,140},{16,272},{20,148},{24,280},{28,15... | collective-permute-start | bytes 393224 | tf_op jit(solution)/shard_map/ppermute | solution.py:189
  35.7 7.3 %collective-permute-start.2 = (bf16[256,256]{1,0:T(8,128)(2,1)S(1)}, bf16[256,256]{1,0:T(8,128)(2,1)S(1)}, u32[]{:S(2)}, u32[]{:S(2)}) collective-permute-start(bf16[256,256]{1,0:T(8,128)(2,1)S(1)} %pad_maximum_fusion.1), channel_id=1, source_target_pairs={{0,64},{4,36},{8,72},{12,44},{16,80},{20,52},{24,88},{28,60},{32,9... | collective-permute-start | bytes 393224 | tf_op jit(solution)/shard_map/ppermute | solution.py:189
  39.1 8.4 %collective-permute-start.3 = (bf16[256,256]{1,0:T(8,128)(2,1)S(1)}, bf16[256,256]{1,0:T(8,128)(2,1)S(1)}, u32[]{:S(2)}, u32[]{:S(2)}) collective-permute-start(bf16[256,256]{1,0:T(8,128)(2,1)S(1)} %pad_maximum_fusion.1), channel_id=1, source_target_pairs={{0,16},{4,12},{8,24},{12,20},{16,32},{20,28},{24,40},{28,36},{32,4... | collective-permute-start | bytes 393224 | tf_op jit(solution)/shard_map/ppermute | solution.py:189
  47.5 3.4 %collective-permute-start.4 = (bf16[512,256]{1,0:T(8,128)(2,1)S(1)}, bf16[512,256]{1,0:T(8,128)(2,1)S(1)}, u32[]{:S(2)}, u32[]{:S(2)}) collective-permute-start(bf16[512,256]{1,0:T(8,128)(2,1)S(1)} %shard_map.88), channel_id=1, source_target_pairs={{0,4},{4,0},{8,12},{12,8},{16,20},{20,16},{24,28},{28,24},{32,36},... | collective-permute-start | bytes 786440 | tf_op jit(solution)/shard_map/ppermute | solution.py:180
  49.4 1.5 %copy-start = (bf16[128,896]{1,0:T(8,128)(2,1)S(1)}, bf16[128,896]{1,0:T(8,128)(2,1)}, u32[]{:S(2)}) copy-start(bf16[128,896]{1,0:T(8,128)(2,1)} %q_ref.1) | copy-start | bytes 688132
  49.4 1.5 %copy-start.1 = (bf16[128,896]{1,0:T(8,128)(2,1)S(1)}, bf16[128,896]{1,0:T(8,128)(2,1)}, u32[]{:S(2)}) copy-start(bf16[128,896]{1,0:T(8,128)(2,1)} %c_ref.1) | copy-start | bytes 688132
  57.2 32.8 %all-to-all-start = ((bf16[4,2,896,128]{3,2,1,0:T(8,128)(2,1)}), bf16[4,2,896,128]{3,2,1,0:T(8,128)(2,1)S(1)}, u32[]{:S(2)}, u32[]{:S(2)}) async-start(bf16[4,2,896,128]{3,2,1,0:T(8,128)(2,1)} %pad_maximum_fusion), calls=%async_computation | async-start | bytes 3670016 | tf_op jit(solution)/shard_map/all_to_all | solution.py:244
  61.4 3.4 %collective-permute-start.5 = (bf16[512,256]{1,0:T(8,128)(2,1)S(1)}, bf16[512,256]{1,0:T(8,128)(2,1)S(1)}, u32[]{:S(2)}, u32[]{:S(2)}) collective-permute-start(bf16[512,256]{1,0:T(8,128)(2,1)S(1)} %get-tuple-element.22), channel_id=1, source_target_pairs={{0,4},{4,0},{8,12},{12,8},{16,20},{20,16},{24,28},{28,24},{32,36},... | collective-permute-start | bytes 786440 | tf_op jit(solution)/shard_map/ppermute | solution.py:180
  64.8 25.0 %collective-permute-start.6 = (bf16[256,256]{1,0:T(8,128)(2,1)S(1)}, bf16[256,256]{1,0:T(8,128)(2,1)S(1)}, u32[]{:S(2)}, u32[]{:S(2)}) collective-permute-start(bf16[256,256]{1,0:T(8,128)(2,1)S(1)} %pad_maximum_fusion.2), channel_id=1, source_target_pairs={{132,4},{140,12},{148,20},{156,28},{164,36},{172,44},{180,52},{188... | collective-permute-start | bytes 393224 | tf_op jit(solution)/shard_map/ppermute | solution.py:189
  66.2 23.7 %collective-permute-start.7 = (bf16[256,256]{1,0:T(8,128)(2,1)S(1)}, bf16[256,256]{1,0:T(8,128)(2,1)S(1)}, u32[]{:S(2)}, u32[]{:S(2)}) collective-permute-start(bf16[256,256]{1,0:T(8,128)(2,1)S(1)} %pad_maximum_fusion.3), channel_id=1, source_target_pairs={{36,4},{44,12},{52,20},{60,28},{64,0},{68,36},{72,8},{76,44},{80,1... | collective-permute-start | bytes 393224 | tf_op jit(solution)/shard_map/ppermute | solution.py:189
  67.5 22.3 %collective-permute-start.8 = (bf16[256,256]{1,0:T(8,128)(2,1)S(1)}, bf16[256,256]{1,0:T(8,128)(2,1)S(1)}, u32[]{:S(2)}, u32[]{:S(2)}) collective-permute-start(bf16[256,256]{1,0:T(8,128)(2,1)S(1)} %pad_maximum_fusion.4), channel_id=1, source_target_pairs={{12,4},{16,0},{20,12},{24,8},{28,20},{32,16},{36,28},{40,24},{44,3... | collective-permute-start | bytes 393224 | tf_op jit(solution)/shard_map/ppermute | solution.py:189
